TPU v7x, 32 devices: a whole 2x2x4 slice. The times are simulated.
32 devices in a mesh: group: 4 (over x, core), sub: 8 (over z, y).
Axes of the slice: x: 2, y: 2, z: 4, core: 2. Of those that a mesh axis runs over, the one named last changes fastest.
Arguments:
- schur: bfloat16 [4, 8, 1024, 1024], P('group', 'sub'), as said below
- local_inverse: bfloat16 [4, 8, 1024, 1024], P('group', 'sub'), as said below
- rhs_parts: bfloat16 [4, 8, 1024, 128], P('group', 'sub'), may hold values from -6 to 6
- basis: bfloat16 [4, 8, 32, 1024], P('group', 'sub'), may hold values from -0.1875 to 0.1875
- coarse_map: int32 [4, 8, 32], P('group', 'sub'), may hold values from 0 to 1023
- coarse_inverse: bfloat16 [4, 1024, 1024], P('group', 'sub'), as said below
- shared_rows: int32 [4, 8, 2, 4, 256], P('group', 'sub'), may hold values from 0 to 1023, as said below
- shared_counts: int32 [4, 8, 4], P('group', 'sub'), may hold values from 0 to 256, as said below
Outputs:
- solution: float32 [4, 8, 1024, 128], P('group', 'sub')
- residual: float32 [4, 8, 1024, 128], P('group', 'sub')
Inputs may be any that keep to these rules, and one draw needn't show every extreme that they name: `schur`: each subdomain matrix is symmetric positive definite. `local_inverse`: each subdomain matrix is symmetric positive definite. `coarse_inverse`: each group's matrix is symmetric positive definite. `shared_rows`: own rows of direction d lie in rows d * 256 to (d + 1) * 256 - 1 and are distinct within a list; the own rows of direction 0 of (g, s) are the partner rows of direction 1 of (g, s + 1) and the reverse, likewise directions 2 and 3 between (g, s) and (g + 1, s); entries past the count are rows of the same block. `shared_counts`: the count of direction 0 of (g, s) equals the count of direction 1 of (g, s + 1), that of direction 2 of (g, s) the count of direction 3 of (g + 1, s); counts are 0 where no neighbour exists; some count equals 256.
All inputs are finite; a program needn't handle non-finite values.
Results may differ from a plain program's by a relative error of at most 0.014.
Values may be sent and summed in bfloat16 or wider, within the bound.
No kernel may reach another device: no remote copies, remote signals or barrier semaphores. Data moves between devices by JAX's collectives and lax.ppermute only.
A program may use at most 64 MiB of HBM per device.

v0:
```python
import jax
import jax.numpy as jnp
from jax import lax
from jax.experimental import pallas as pl
from jax.experimental.pallas import tpu as pltpu
from jax.sharding import PartitionSpec as P

ITERS = 3
HIGHEST = lax.Precision.HIGHEST


def halves(x):
    high = lax.reduce_precision(x, 8, 7)
    return jnp.concatenate([high, x - high], axis=-1).astype(jnp.bfloat16)


def times(matrix, x):
    both = jnp.dot(matrix, halves(x), preferred_element_type=jnp.float32)
    n = x.shape[-1]
    return both[:, :n] + both[:, n:]


def times_t(matrix, x):
    both = lax.dot_general(
        matrix, halves(x), (((0,), (0,)), ((), ())), preferred_element_type=jnp.float32
    )
    n = x.shape[-1]
    return both[:, :n] + both[:, n:]


def swap(x, axis, bit):
    return lax.ppermute(x, axis, [(i, i ^ bit) for i in range(lax.axis_size(axis))])


def bits_of(axis):
    count = lax.axis_size(axis)
    if count & (count - 1):
        raise ValueError("axis size")
    return [1 << b for b in range(count.bit_length() - 1)]


def total(x):
    group_bits, sub_bits = bits_of("group"), bits_of("sub")
    order = []
    for i in range(max(len(group_bits), len(sub_bits))):
        if i < len(group_bits):
            order.append(("group", group_bits[i]))
        if i < len(sub_bits):
            order.append(("sub", sub_bits[i]))
    for axis, bit in order:
        x = x + swap(x, axis, bit)
    return x


def gather_sub(x):
    count = lax.axis_size("sub")
    copies = jnp.broadcast_to(x[None], (count,) + x.shape)
    out = lax.all_to_all(copies, "sub", 0, 0)
    return out.reshape((-1,) + x.shape[1:])


def one_hot(rows, count):
    return rows[:, None] == jnp.arange(count, dtype=jnp.int32)[None, :]


def selected_inverse(coarse_map, inverse_rows):
    modes = coarse_map.shape[0]
    rows_here, coarse_total = inverse_rows.shape
    maps = gather_sub(coarse_map)
    count = maps.shape[0] // modes
    columns = one_hot(maps, coarse_total).astype(jnp.bfloat16)
    picked_columns = lax.dot_general(
        inverse_rows, columns, (((1,), (1,)), ((), ())), preferred_element_type=jnp.float32
    ).astype(jnp.bfloat16)
    first = lax.axis_index("sub") * rows_here
    rows = one_hot(maps - first, rows_here).astype(jnp.bfloat16)
    table = jnp.dot(rows, picked_columns, preferred_element_type=jnp.float32).astype(jnp.bfloat16)
    table = table.reshape(count, modes, count * modes)
    return lax.all_to_all(table, "sub", 0, 0).sum(axis=0)


def eliminate(matrix, block, tile=8):
    n, width = matrix.shape[0], block.shape[1]
    sublane = lax.broadcasted_iota(jnp.int32, (tile, 1), 0)
    left = [matrix[i : i + tile] for i in range(0, n, tile)]
    right = [block[i : i + tile] for i in range(0, n, tile)]
    for k in range(n // tile):
        pivot_left, pivot_right = left[k], right[k]
        at = k * tile
        spread = [
            jnp.broadcast_to(pivot_left[:, at + j : at + j + 1], (tile, n)) for j in range(tile)
        ]
        for j in range(tile):
            inverse = 1.0 / spread[j][j : j + 1]
            here = sublane == j
            column = spread[j]

            def cleared(rows, column=column, inverse=inverse, here=here, j=j):
                pivot = rows[j : j + 1] * inverse
                return jnp.where(here, pivot, rows - column * pivot)

            for i in range(j + 1, tile):
                spread[i] = cleared(spread[i])
            pivot_left, pivot_right = cleared(pivot_left), cleared(pivot_right)
        for i in range(n // tile):
            if i == k:
                continue
            old = left[i]
            new_left, new_right = old, right[i]
            for j in range(tile):
                scale = jnp.broadcast_to(old[:, at + j : at + j + 1], (tile, n))
                new_left = new_left - scale * pivot_left[j : j + 1]
                new_right = new_right - scale * pivot_right[j : j + 1]
            left[i], right[i] = new_left, new_right
        left[k], right[k] = pivot_left, pivot_right
    return jnp.concatenate(right, axis=0)


def exact(a, b):
    return jnp.dot(a, b, precision=HIGHEST, preferred_element_type=jnp.float32)


def symmetric(a):
    return (a + a.T) * 0.5


def first_step_kernel(grams, alpha):
    n = alpha.shape[0]
    alpha[...] = eliminate(symmetric(grams[:, n:]), grams[:, :n])


def next_step_kernel(grams, inner_inverse, curvature_old, alpha, beta, curvature):
    n = alpha.shape[0]
    mixing = exact(inner_inverse[...], grams[:, :n])
    bent = grams[:, n:] - exact(mixing.T, exact(curvature_old[...], mixing))
    beta[...] = mixing
    curvature[...] = bent
    alpha[...] = eliminate(symmetric(bent), grams[:, :n])


def inverse_kernel(grams, out):
    n = out.shape[0]
    rows = lax.broadcasted_iota(jnp.int32, (n, n), 0)
    columns = lax.broadcasted_iota(jnp.int32, (n, n), 1)
    out[...] = eliminate(symmetric(grams[:, :n]), (rows == columns).astype(jnp.float32))


def small(kernel, count, name, *args):
    n = args[0].shape[0]
    square = jax.ShapeDtypeStruct((n, n), jnp.float32)
    return pl.pallas_call(
        kernel,
        out_shape=[square] * count,
        name=name,
        cost_estimate=pl.CostEstimate(flops=8 * n**3, bytes_accessed=6 * 4 * n * n, transcendentals=0),
    )(*args)


def neighbour_tables(rows, counts):
    own, partner = rows[0], rows[1]
    capacity = own.shape[1]

    def table(d, zone):
        live = jnp.arange(capacity, dtype=jnp.int32)[:, None] < counts[d]
        to = (one_hot(own[d] - d * capacity, capacity) & live).astype(jnp.bfloat16)
        source = one_hot(partner[d] - zone * capacity, capacity).astype(jnp.bfloat16)
        return lax.dot_general(
            to, source, (((0,), (0,)), ((), ())), preferred_element_type=jnp.float32
        )

    return [table(d, d ^ 1) for d in range(4)]


def line(axis, step):
    count = lax.axis_size(axis)
    return [(i, i + step) for i in range(count) if 0 <= i + step < count]


def shards(
    schur, local_inverse, rhs_parts, basis, coarse_map, coarse_inverse, shared_rows, shared_counts
):
    schur, local_inverse, basis = schur[0, 0], local_inverse[0, 0], basis[0, 0]
    rhs = rhs_parts[0, 0].astype(jnp.float32)
    zone = shared_rows.shape[-1]
    columns = rhs.shape[1]
    tables = neighbour_tables(shared_rows[0, 0], shared_counts[0, 0])
    weight = 1.0 / (1.0 + jnp.concatenate([t.sum(axis=1) for t in tables]))[:, None]
    tables = [t.astype(jnp.bfloat16) for t in tables]
    chosen = selected_inverse(coarse_map[0, 0], coarse_inverse[0])

    def assemble(block):
        received = [
            lax.ppermute(block[(d ^ 1) * zone : ((d ^ 1) + 1) * zone], axis, line(axis, step))
            for d, (axis, step) in enumerate(
                (("sub", -1), ("sub", 1), ("group", -1), ("group", 1))
            )
        ]
        return block + jnp.concatenate([times(t, r) for t, r in zip(tables, received)], axis=0)

    def precondition(block):
        scaled = weight * block
        coarse = gather_sub(times(basis, scaled))
        local = times(local_inverse, scaled)
        picked = times(chosen, coarse)
        return assemble(weight * (local + times_t(basis, picked)))

    def operator(block):
        return assemble(times(schur, block))

    def mix(block, mixing):
        return jnp.dot(block, mixing, precision=HIGHEST)

    r = assemble(rhs)
    z = precondition(r)
    w = operator(z)
    x = None
    for iteration in range(ITERS):
        last = iteration + 1 == ITERS
        grams = total(
            lax.dot_general(
                weight * z,
                jnp.concatenate([r, w], axis=1),
                (((0,), (0,)), ((), ())),
                precision=HIGHEST,
            )
        )
        if not last:
            m = precondition(w)
            n = operator(m)
        if iteration == 0:
            (alpha,) = small(first_step_kernel, 1, "first_step", grams)
            curvature = grams[:, columns:]
            p, s = z, w
            if not last:
                q, t = m, n
        else:
            alpha, beta, curvature = small(
                next_step_kernel, 3, "next_step", grams, inner_inverse, curvature
            )
            p, s = z + mix(p, beta), w + mix(s, beta)
            if not last:
                q, t = m + mix(q, beta), n + mix(t, beta)
        x = mix(p, alpha) if x is None else x + mix(p, alpha)
        r = r - mix(s, alpha)
        if not last:
            z, w = z - mix(q, alpha), w - mix(t, alpha)
            (inner_inverse,) = small(inverse_kernel, 1, "inverse", grams)
    return x[None, None], r[None, None]


def solution(mesh):
    placed = (
        P("group", "sub", None, None),
        P("group", "sub", None, None),
        P("group", "sub", None, None),
        P("group", "sub", None, None),
        P("group", "sub", None),
        P("group", "sub", None),
        P("group", "sub", None, None, None),
        P("group", "sub", None),
    )
    return jax.shard_map(
        shards,
        mesh=mesh,
        in_specs=placed,
        out_specs=(P("group", "sub", None, None), P("group", "sub", None, None)),
        check_vma=False,
    )
```

profile of v0, /device:TPU:0, one launch (start us, length us, event | category | flops | bytes accessed | tf_op | source)
XLA Modules:
  0.0 291.8 jit_solution(14304216155671274897)
XLA Ops:
  3.8 5.5 %collective-permute-start.1 = (f32[256,128]{1,0:T(8,128)}, f32[256,128]{1,0:T(8,128)S(1)}, u32[]{:S(2)}, u32[]{:S(2)}) collective-permute-start(f32[256,128]{1,0:T(8,128)} %get-tuple-element.50), channel_id=1, source_target_pairs={{0,1},{1,2},{2,3},{3,4},{4,5},{5,6},{6,7},{8,9},{9,10},{10,11},{11... | collective-permute-start | bytes 393224 | tf_op jit(solution)/shard_map/ppermute | solution.py:193
  10.6 3.7 %collective-permute-start.3 = (f32[256,128]{1,0:T(8,128)}, f32[256,128]{1,0:T(8,128)}, u32[]{:S(2)}, u32[]{:S(2)}) collective-permute-start(f32[256,128]{1,0:T(8,128)} %get-tuple-element.51), channel_id=1, source_target_pairs={{0,8},{8,16},{16,24},{1,9},{9,17},{17,25},{2,10},{10,18},{18,26},{... | collective-permute-start | bytes 393224 | tf_op jit(solution)/shard_map/ppermute | solution.py:193
  15.6 6.2 %all-to-all-start = ((s32[8,1,32]{2,1,0:T(1,128)}), s32[8,1,32]{2,1,0:T(1,128)S(1)}, u32[]{:S(2)}, u32[]{:S(2)}) async-start(s32[8,1,32]{2,1,0:T(1,128)} %broadcast_in_dim.12), calls=%async_computation | async-start | bytes 8192 | tf_op jit(solution)/shard_map/all_to_all | solution.py:58
  22.6 1.4 fusion.334
  30.8 5.8 %all-to-all-start.1 = ((bf16[8,32,256]{2,1,0:T(8,128)(2,1)}), bf16[8,32,256]{2,1,0:T(8,128)(2,1)S(1)}, u32[]{:S(2)}, u32[]{:S(2)}) async-start(bf16[8,32,256]{2,1,0:T(8,128)(2,1)} %bitcast.21), calls=%async_computation.1 | async-start | bytes 262144 | tf_op jit(solution)/shard_map/all_to_all | solution.py:79
  41.1 2.9 all-to-all-done.1
  44.7 3.4 %all-to-all-start.2 = ((f32[8,32,128]{2,1,0:T(8,128)}), f32[8,32,128]{2,1,0:T(8,128)S(1)}, u32[]{:S(2)}, u32[]{:S(2)}) async-start(f32[8,32,128]{2,1,0:T(8,128)} %broadcast_in_dim.13), calls=%async_computation.2 | async-start | bytes 262144 | tf_op jit(solution)/shard_map/all_to_all | solution.py:58
  48.0 2.7 fusion.18
  50.7 4.6 %all-to-all-done.2 = f32[8,32,128]{2,1,0:T(8,128)S(1)} async-done(((f32[8,32,128]{2,1,0:T(8,128)}), f32[8,32,128]{2,1,0:T(8,128)S(1)}, u32[]{:S(2)}, u32[]{:S(2)}) %all-to-all-start.2) | async-done | bytes 131104 | tf_op jit(solution)/shard_map/all_to_all | solution.py:58
  58.1 4.6 %collective-permute-start.5 = (f32[256,128]{1,0:T(8,128)S(1)}, f32[256,128]{1,0:T(8,128)S(1)}, u32[]{:S(2)}, u32[]{:S(2)}) collective-permute-start(f32[256,128]{1,0:T(8,128)S(1)} %get-tuple-element.47), channel_id=1, source_target_pairs={{0,1},{1,2},{2,3},{3,4},{4,5},{5,6},{6,7},{8,9},{9,10},{10,11},{11... | collective-permute-start | bytes 393224 | tf_op jit(solution)/shard_map/ppermute | solution.py:193
  64.0 3.0 %collective-permute-start.7 = (f32[256,128]{1,0:T(8,128)S(1)}, f32[256,128]{1,0:T(8,128)S(1)}, u32[]{:S(2)}, u32[]{:S(2)}) collective-permute-start(f32[256,128]{1,0:T(8,128)S(1)} %get-tuple-element.45), channel_id=1, source_target_pairs={{0,8},{8,16},{16,24},{1,9},{9,17},{17,25},{2,10},{10,18},{18,26},{... | collective-permute-start | bytes 393224 | tf_op jit(solution)/shard_map/ppermute | solution.py:193
  71.6 4.6 %collective-permute-start.9 = (f32[256,128]{1,0:T(8,128)S(1)}, f32[256,128]{1,0:T(8,128)S(1)}, u32[]{:S(2)}, u32[]{:S(2)}) collective-permute-start(f32[256,128]{1,0:T(8,128)S(1)} %get-tuple-element.43), channel_id=1, source_target_pairs={{0,1},{1,2},{2,3},{3,4},{4,5},{5,6},{6,7},{8,9},{9,10},{10,11},{11... | collective-permute-start | bytes 393224 | tf_op jit(solution)/shard_map/ppermute | solution.py:193
  77.5 3.2 %collective-permute-start.11 = (f32[256,128]{1,0:T(8,128)S(1)}, f32[256,128]{1,0:T(8,128)S(1)}, u32[]{:S(2)}, u32[]{:S(2)}) collective-permute-start(f32[256,128]{1,0:T(8,128)S(1)} %get-tuple-element.41), channel_id=1, source_target_pairs={{0,8},{8,16},{16,24},{1,9},{9,17},{17,25},{2,10},{10,18},{18,26},{... | collective-permute-start | bytes 393224 | tf_op jit(solution)/shard_map/ppermute | solution.py:193
  82.6 1.9 fusion.33
  84.7 3.4 %collective-permute-start.12 = (f32[128,256]{1,0:T(8,128)}, f32[128,256]{1,0:T(8,128)}, u32[]{:S(2)}, u32[]{:S(2)}) collective-permute-start(f32[128,256]{1,0:T(8,128)} %fusion.33), channel_id=1, source_target_pairs={{0,8},{8,0},{16,24},{24,16},{1,9},{9,1},{17,25},{25,17},{2,10},{10... | collective-permute-start | bytes 393224 | tf_op jit(solution)/shard_map/ppermute | solution.py:32
  89.0 4.0 %all-to-all-start.3 = ((f32[8,32,128]{2,1,0:T(8,128)}), f32[8,32,128]{2,1,0:T(8,128)}, u32[]{:S(2)}, u32[]{:S(2)}) async-start(f32[8,32,128]{2,1,0:T(8,128)} %broadcast_in_dim.14), calls=%async_computation.3 | async-start | bytes 262144 | tf_op jit(solution)/shard_map/all_to_all | solution.py:58
  93.0 2.7 fusion.15
  95.7 1.6 add.294
  97.4 1.9 collective-permute-start.13
  99.3 1.5 all-to-all-done.3
  105.5 4.6 %collective-permute-start.18 = (f32[256,128]{1,0:T(8,128)S(1)}, f32[256,128]{1,0:T(8,128)S(1)}, u32[]{:S(2)}, u32[]{:S(2)}) collective-permute-start(f32[256,128]{1,0:T(8,128)S(1)} %get-tuple-element.39), channel_id=1, source_target_pairs={{0,1},{1,2},{2,3},{3,4},{4,5},{5,6},{6,7},{8,9},{9,10},{10,11},{11... | collective-permute-start | bytes 393224 | tf_op jit(solution)/shard_map/ppermute | solution.py:193
  110.1 1.3 collective-permute-start.19
  111.4 15.2 %collective-permute-start.20 = (f32[256,128]{1,0:T(8,128)S(1)}, f32[256,128]{1,0:T(8,128)S(1)}, u32[]{:S(2)}, u32[]{:S(2)}) collective-permute-start(f32[256,128]{1,0:T(8,128)S(1)} %get-tuple-element.37), channel_id=1, source_target_pairs={{0,8},{8,16},{16,24},{1,9},{9,17},{17,25},{2,10},{10,18},{18,26},{... | collective-permute-start | bytes 393224 | tf_op jit(solution)/shard_map/ppermute | solution.py:193
  127.6 2.5 collective-permute-start.14
  134.9 4.6 %collective-permute-start.22 = (f32[256,128]{0,1:T(8,128)S(1)}, f32[256,128]{0,1:T(8,128)S(1)}, u32[]{:S(2)}, u32[]{:S(2)}) collective-permute-start(f32[256,128]{0,1:T(8,128)S(1)} %get-tuple-element.35), channel_id=1, source_target_pairs={{0,1},{1,2},{2,3},{3,4},{4,5},{5,6},{6,7},{8,9},{9,10},{10,11},{11... | collective-permute-start | bytes 393224 | tf_op jit(solution)/shard_map/ppermute | solution.py:193
  140.8 3.0 %collective-permute-start.24 = (f32[256,128]{0,1:T(8,128)S(1)}, f32[256,128]{0,1:T(8,128)S(1)}, u32[]{:S(2)}, u32[]{:S(2)}) collective-permute-start(f32[256,128]{0,1:T(8,128)S(1)} %get-tuple-element.33), channel_id=1, source_target_pairs={{0,8},{8,16},{16,24},{1,9},{9,17},{17,25},{2,10},{10,18},{18,26},{... | collective-permute-start | bytes 393224 | tf_op jit(solution)/shard_map/ppermute | solution.py:193
  147.5 2.1 collective-permute-done.15
  149.6 1.4 collective-permute-start.16
  151.7 6.6 %collective-permute-done.16 = f32[128,256]{1,0:T(8,128)S(1)} collective-permute-done((f32[128,256]{1,0:T(8,128)S(1)}, f32[128,256]{1,0:T(8,128)S(1)}, u32[]{:S(2)}, u32[]{:S(2)}) %collective-permute-start.16) | collective-permute-done | bytes 131104 | tf_op jit(solution)/shard_map/ppermute | solution.py:32
  159.0 5.5 %first_step.1 = f32[128,128]{1,0:T(8,128)} custom-call(f32[128,256]{1,0:T(8,128)} %add.298.grams), custom_call_target="tpu_custom_call" | custom-call | flops 16777216 | bytes 393216 | tf_op jit(solution)/shard_map/first_step/pallas_call | solution.py:151
  164.5 1.7 convolution_subtract_fusion.5
  166.2 1.8 convolution_subtract_fusion.6
  169.2 1.9 fusion.37
  172.0 4.2 %all-to-all-start.4 = ((f32[8,32,128]{2,1,0:T(8,128)}), f32[8,32,128]{2,1,0:T(8,128)}, u32[]{:S(2)}, u32[]{:S(2)}) async-start(f32[8,32,128]{2,1,0:T(8,128)} %broadcast_in_dim.15), calls=%async_computation.4 | async-start | bytes 262144 | tf_op jit(solution)/shard_map/all_to_all | solution.py:58
  176.2 2.7 fusion.12
  178.9 1.6 add.315
  180.6 2.0 collective-permute-start.26
  182.6 1.3 all-to-all-done.4
  187.3 1.3 collective-permute-start.30
  188.6 4.6 %collective-permute-start.31 = (f32[256,128]{1,0:T(8,128)S(1)}, f32[256,128]{1,0:T(8,128)S(1)}, u32[]{:S(2)}, u32[]{:S(2)}) collective-permute-start(f32[256,128]{1,0:T(8,128)S(1)} %get-tuple-element.31), channel_id=1, source_target_pairs={{0,1},{1,2},{2,3},{3,4},{4,5},{5,6},{6,7},{8,9},{9,10},{10,11},{11... | collective-permute-start | bytes 393224 | tf_op jit(solution)/shard_map/ppermute | solution.py:193
  193.2 1.3 collective-permute-start.32
  194.5 3.0 %collective-permute-start.33 = (f32[256,128]{1,0:T(8,128)S(1)}, f32[256,128]{1,0:T(8,128)S(1)}, u32[]{:S(2)}, u32[]{:S(2)}) collective-permute-start(f32[256,128]{1,0:T(8,128)S(1)} %get-tuple-element.29), channel_id=1, source_target_pairs={{0,8},{8,16},{16,24},{1,9},{9,17},{17,25},{2,10},{10,18},{18,26},{... | collective-permute-start | bytes 393224 | tf_op jit(solution)/shard_map/ppermute | solution.py:193
  197.5 1.6 add.316
  205.9 5.5 %inverse.2.inner_inverse = f32[128,128]{1,0:T(8,128)} custom-call(f32[128,256]{1,0:T(8,128)} %add.298.grams), custom_call_target="tpu_custom_call" | custom-call | flops 16777216 | bytes 393216 | tf_op jit(solution)/shard_map/inverse/pallas_call | solution.py:151
  211.3 4.5 %collective-permute-start.35 = (f32[256,128]{0,1:T(8,128)}, f32[256,128]{0,1:T(8,128)S(1)}, u32[]{:S(2)}, u32[]{:S(2)}) collective-permute-start(f32[256,128]{0,1:T(8,128)} %get-tuple-element.27), channel_id=1, source_target_pairs={{0,1},{1,2},{2,3},{3,4},{4,5},{5,6},{6,7},{8,9},{9,10},{10,11},{11... | collective-permute-start | bytes 393224 | tf_op jit(solution)/shard_map/ppermute | solution.py:193
  217.2 3.4 %collective-permute-start.37 = (f32[256,128]{0,1:T(8,128)}, f32[256,128]{0,1:T(8,128)S(1)}, u32[]{:S(2)}, u32[]{:S(2)}) collective-permute-start(f32[256,128]{0,1:T(8,128)} %get-tuple-element.25), channel_id=1, source_target_pairs={{0,8},{8,16},{16,24},{1,9},{9,17},{17,25},{2,10},{10,18},{18,26},{... | collective-permute-start | bytes 393224 | tf_op jit(solution)/shard_map/ppermute | solution.py:193
  227.5 2.3 collective-permute-start.29
  230.5 7.0 %collective-permute-done.29 = f32[128,256]{1,0:T(8,128)S(1)} collective-permute-done((f32[128,256]{1,0:T(8,128)S(1)}, f32[128,256]{1,0:T(8,128)S(1)}, u32[]{:S(2)}, u32[]{:S(2)}) %collective-permute-start.29) | collective-permute-done | bytes 131104 | tf_op jit(solution)/shard_map/ppermute | solution.py:32
  238.2 6.1 %next_step.2 = (f32[128,128]{1,0:T(8,128)}, f32[128,128]{1,0:T(8,128)}, f32[128,128]{1,0:T(8,128)}) custom-call(f32[128,256]{1,0:T(8,128)} %add.319.grams, f32[128,128]{1,0:T(8,128)} %inverse.2.inner_inverse, f32[128,128]{1,0:T(8,128)} %slice.628.curvature_old), custom_call_target="tpu_custom_call" | custom-call | flops 16777216 | bytes 393216 | tf_op jit(solution)/shard_map/next_step/pallas_call | solution.py:151
  244.2 1.7 convolution_add_fusion.3
  246.1 2.1 convolution_add_fusion.4
  252.5 1.3 collective-permute-done.38
  253.9 1.9 collective-permute-start.39
  255.8 3.8 %collective-permute-done.39 = f32[128,256]{1,0:T(8,128)S(1)} collective-permute-done((f32[128,256]{1,0:T(8,128)S(1)}, f32[128,256]{1,0:T(8,128)S(1)}, u32[]{:S(2)}, u32[]{:S(2)}) %collective-permute-start.39) | collective-permute-done | bytes 131104 | tf_op jit(solution)/shard_map/ppermute | solution.py:32
  260.1 4.5 %collective-permute-done.40 = f32[128,256]{1,0:T(8,128)S(1)} collective-permute-done((f32[128,256]{1,0:T(8,128)S(1)}, f32[128,256]{1,0:T(8,128)S(1)}, u32[]{:S(2)}, u32[]{:S(2)}) %collective-permute-start.40) | collective-permute-done | bytes 131104 | tf_op jit(solution)/shard_map/ppermute | solution.py:32
  264.8 1.4 convolution_add_fusion.5
  266.1 5.6 %inverse.3.inner_inverse = f32[128,128]{1,0:T(8,128)} custom-call(f32[128,256]{1,0:T(8,128)} %add.319.grams), custom_call_target="tpu_custom_call" | custom-call | flops 16777216 | bytes 393216 | tf_op jit(solution)/shard_map/inverse/pallas_call | solution.py:151
  271.8 2.8 collective-permute-start.42
  274.6 2.4 fusion.335
  278.5 6.1 %next_step.3 = (f32[128,128]{1,0:T(8,128)}, f32[128,128]{1,0:T(8,128)}, f32[128,128]{1,0:T(8,128)}) custom-call(f32[128,256]{1,0:T(8,128)} %add.345.grams, f32[128,128]{1,0:T(8,128)} %inverse.3.inner_inverse, f32[128,128]{1,0:T(8,128)} %get-tuple-element.9.curvature_old), custom_call_target="tpu_custom_call" | custom-call | flops 16777216 | bytes 393216 | tf_op jit(solution)/shard_map/next_step/pallas_call | solution.py:151
  284.6 1.7 convolution_add_fusion
  286.3 1.9 convolution_add_fusion.1
  288.2 1.4 fusion.30
  290.2 1.4 fusion.32
  (356 shorter events, 75.2 us)
Async XLA Ops:
  0.6 47.4 %copy-start = (bf16[1,1,1024,1024]{3,2,1,0:T(8,128)(2,1)S(1)}, bf16[1,1,1024,1024]{3,2,1,0:T(8,128)(2,1)}, u32[]{:S(2)}) copy-start(bf16[1,1,1024,1024]{3,2,1,0:T(8,128)(2,1)} %param.9) | copy-start | bytes 6291460
  0.6 29.0 %copy-start.66 = (bf16[1,128,1024]{2,1,0:T(8,128)(2,1)S(1)}, bf16[1,128,1024]{2,1,0:T(8,128)(2,1)}, u32[]{:S(2)}) copy-start(bf16[1,128,1024]{2,1,0:T(8,128)(2,1)} %param.13) | copy-start | bytes 786436
  2.5 34.1 %collective-permute-start = (f32[256,128]{1,0:T(8,128)S(1)}, f32[256,128]{1,0:T(8,128)S(1)}, u32[]{:S(2)}, u32[]{:S(2)}) collective-permute-start(f32[256,128]{1,0:T(8,128)S(1)} %get-tuple-element.48), channel_id=1, source_target_pairs={{1,0},{2,1},{3,2},{4,3},{5,4},{6,5},{7,6},{9,8},{10,9},{11,10},{12... | collective-permute-start | bytes 393224 | tf_op jit(solution)/shard_map/ppermute | solution.py:193
  3.8 33.1 %collective-permute-start.1 = (f32[256,128]{1,0:T(8,128)}, f32[256,128]{1,0:T(8,128)S(1)}, u32[]{:S(2)}, u32[]{:S(2)}) collective-permute-start(f32[256,128]{1,0:T(8,128)} %get-tuple-element.50), channel_id=1, source_target_pairs={{0,1},{1,2},{2,3},{3,4},{4,5},{5,6},{6,7},{8,9},{9,10},{10,11},{11... | collective-permute-start | bytes 393224 | tf_op jit(solution)/shard_map/ppermute | solution.py:193
  9.3 27.9 %collective-permute-start.2 = (f32[256,128]{1,0:T(8,128)S(1)}, f32[256,128]{1,0:T(8,128)}, u32[]{:S(2)}, u32[]{:S(2)}) collective-permute-start(f32[256,128]{1,0:T(8,128)S(1)} %get-tuple-element.49), channel_id=1, source_target_pairs={{8,0},{16,8},{24,16},{9,1},{17,9},{25,17},{10,2},{18,10},{26,18},{... | collective-permute-start | bytes 393224 | tf_op jit(solution)/shard_map/ppermute | solution.py:193
  10.6 27.8 %collective-permute-start.3 = (f32[256,128]{1,0:T(8,128)}, f32[256,128]{1,0:T(8,128)}, u32[]{:S(2)}, u32[]{:S(2)}) collective-permute-start(f32[256,128]{1,0:T(8,128)} %get-tuple-element.51), channel_id=1, source_target_pairs={{0,8},{8,16},{16,24},{1,9},{9,17},{17,25},{2,10},{10,18},{18,26},{... | collective-permute-start | bytes 393224 | tf_op jit(solution)/shard_map/ppermute | solution.py:193
  15.6 12.7 %all-to-all-start = ((s32[8,1,32]{2,1,0:T(1,128)}), s32[8,1,32]{2,1,0:T(1,128)S(1)}, u32[]{:S(2)}, u32[]{:S(2)}) async-start(s32[8,1,32]{2,1,0:T(1,128)} %broadcast_in_dim.12), calls=%async_computation | async-start | bytes 8192 | tf_op jit(solution)/shard_map/all_to_all | solution.py:58
  26.9 53.8 %copy-start.15 = (bf16[256,256]{0,1:T(8,128)(2,1)}, bf16[256,256]{0,1:T(8,128)(2,1)S(1)}, u32[]{:S(2)}) copy-start(bf16[256,256]{0,1:T(8,128)(2,1)S(1)} %get-tuple-element.52) | copy-start | bytes 393220
  30.8 13.2 %all-to-all-start.1 = ((bf16[8,32,256]{2,1,0:T(8,128)(2,1)}), bf16[8,32,256]{2,1,0:T(8,128)(2,1)S(1)}, u32[]{:S(2)}, u32[]{:S(2)}) async-start(bf16[8,32,256]{2,1,0:T(8,128)(2,1)} %bitcast.21), calls=%async_computation.1 | async-start | bytes 262144 | tf_op jit(solution)/shard_map/all_to_all | solution.py:79
  39.9 4.8 %copy-start.62 = (bf16[1024,128]{1,0:T(8,128)(2,1)}, bf16[1024,128]{1,0:T(8,128)(2,1)S(1)}, u32[]{:S(2)}) copy-start(bf16[1024,128]{1,0:T(8,128)(2,1)S(1)} %get-tuple-element.18) | copy-start | bytes 786436
  44.7 10.7 %all-to-all-start.2 = ((f32[8,32,128]{2,1,0:T(8,128)}), f32[8,32,128]{2,1,0:T(8,128)S(1)}, u32[]{:S(2)}, u32[]{:S(2)}) async-start(f32[8,32,128]{2,1,0:T(8,128)} %broadcast_in_dim.13), calls=%async_computation.2 | async-start | bytes 262144 | tf_op jit(solution)/shard_map/all_to_all | solution.py:58
  50.7 6.0 %copy-start.65 = (bf16[32,256]{1,0:T(8,128)(2,1)}, bf16[32,256]{1,0:T(8,128)(2,1)S(1)}, u32[]{:S(2)}) copy-start(bf16[32,256]{1,0:T(8,128)(2,1)S(1)} %reduce_sum.52) | copy-start | bytes 49156
  56.8 10.2 %collective-permute-start.4 = (f32[256,128]{1,0:T(8,128)S(1)}, f32[256,128]{1,0:T(8,128)S(1)}, u32[]{:S(2)}, u32[]{:S(2)}) collective-permute-start(f32[256,128]{1,0:T(8,128)S(1)} %get-tuple-element.44), channel_id=1, source_target_pairs={{1,0},{2,1},{3,2},{4,3},{5,4},{6,5},{7,6},{9,8},{10,9},{11,10},{12... | collective-permute-start | bytes 393224 | tf_op jit(solution)/shard_map/ppermute | solution.py:193
  58.1 9.2 %collective-permute-start.5 = (f32[256,128]{1,0:T(8,128)S(1)}, f32[256,128]{1,0:T(8,128)S(1)}, u32[]{:S(2)}, u32[]{:S(2)}) collective-permute-start(f32[256,128]{1,0:T(8,128)S(1)} %get-tuple-element.47), channel_id=1, source_target_pairs={{0,1},{1,2},{2,3},{3,4},{4,5},{5,6},{6,7},{8,9},{9,10},{10,11},{11... | collective-permute-start | bytes 393224 | tf_op jit(solution)/shard_map/ppermute | solution.py:193
  62.7 4.9 %collective-permute-start.6 = (f32[256,128]{1,0:T(8,128)S(1)}, f32[256,128]{1,0:T(8,128)S(1)}, u32[]{:S(2)}, u32[]{:S(2)}) collective-permute-start(f32[256,128]{1,0:T(8,128)S(1)} %get-tuple-element.46), channel_id=1, source_target_pairs={{8,0},{16,8},{24,16},{9,1},{17,9},{25,17},{10,2},{18,10},{26,18},{... | collective-permute-start | bytes 393224 | tf_op jit(solution)/shard_map/ppermute | solution.py:193
  64.0 4.0 %collective-permute-start.7 = (f32[256,128]{1,0:T(8,128)S(1)}, f32[256,128]{1,0:T(8,128)S(1)}, u32[]{:S(2)}, u32[]{:S(2)}) collective-permute-start(f32[256,128]{1,0:T(8,128)S(1)} %get-tuple-element.45), channel_id=1, source_target_pairs={{0,8},{8,16},{16,24},{1,9},{9,17},{17,25},{2,10},{10,18},{18,26},{... | collective-permute-start | bytes 393224 | tf_op jit(solution)/shard_map/ppermute | solution.py:193
  70.3 10.4 %collective-permute-start.8 = (f32[256,128]{1,0:T(8,128)S(1)}, f32[256,128]{1,0:T(8,128)S(1)}, u32[]{:S(2)}, u32[]{:S(2)}) collective-permute-start(f32[256,128]{1,0:T(8,128)S(1)} %get-tuple-element.40), channel_id=1, source_target_pairs={{1,0},{2,1},{3,2},{4,3},{5,4},{6,5},{7,6},{9,8},{10,9},{11,10},{12... | collective-permute-start | bytes 393224 | tf_op jit(solution)/shard_map/ppermute | solution.py:193
  71.6 9.4 %collective-permute-start.9 = (f32[256,128]{1,0:T(8,128)S(1)}, f32[256,128]{1,0:T(8,128)S(1)}, u32[]{:S(2)}, u32[]{:S(2)}) collective-permute-start(f32[256,128]{1,0:T(8,128)S(1)} %get-tuple-element.43), channel_id=1, source_target_pairs={{0,1},{1,2},{2,3},{3,4},{4,5},{5,6},{6,7},{8,9},{9,10},{10,11},{11... | collective-permute-start | bytes 393224 | tf_op jit(solution)/shard_map/ppermute | solution.py:193
  76.2 5.1 %collective-permute-start.10 = (f32[256,128]{1,0:T(8,128)S(1)}, f32[256,128]{1,0:T(8,128)S(1)}, u32[]{:S(2)}, u32[]{:S(2)}) collective-permute-start(f32[256,128]{1,0:T(8,128)S(1)} %get-tuple-element.42), channel_id=1, source_target_pairs={{8,0},{16,8},{24,16},{9,1},{17,9},{25,17},{10,2},{18,10},{26,18},{... | collective-permute-start | bytes 393224 | tf_op jit(solution)/shard_map/ppermute | solution.py:193
  77.5 4.2 %collective-permute-start.11 = (f32[256,128]{1,0:T(8,128)S(1)}, f32[256,128]{1,0:T(8,128)S(1)}, u32[]{:S(2)}, u32[]{:S(2)}) collective-permute-start(f32[256,128]{1,0:T(8,128)S(1)} %get-tuple-element.41), channel_id=1, source_target_pairs={{0,8},{8,16},{16,24},{1,9},{9,17},{17,25},{2,10},{10,18},{18,26},{... | collective-permute-start | bytes 393224 | tf_op jit(solution)/shard_map/ppermute | solution.py:193
  81.9 6.2 %copy-start.53 = (bf16[1,1,32,1024]{3,2,1,0:T(8,128)(2,1)S(1)}, bf16[1,1,32,1024]{3,2,1,0:T(8,128)(2,1)}, u32[]{:S(2)}) copy-start(bf16[1,1,32,1024]{3,2,1,0:T(8,128)(2,1)} %param.11) | copy-start | bytes 196612
  82.1 6.2 %copy-start.59 = (bf16[1024,128]{1,0:T(8,128)(2,1)}, bf16[1024,128]{1,0:T(8,128)(2,1)S(1)}, u32[]{:S(2)}) copy-start(bf16[1024,128]{1,0:T(8,128)(2,1)S(1)} %get-tuple-element.14) | copy-start | bytes 786436
  84.7 11.1 %collective-permute-start.12 = (f32[128,256]{1,0:T(8,128)}, f32[128,256]{1,0:T(8,128)}, u32[]{:S(2)}, u32[]{:S(2)}) collective-permute-start(f32[128,256]{1,0:T(8,128)} %fusion.33), channel_id=1, source_target_pairs={{0,8},{8,0},{16,24},{24,16},{1,9},{9,1},{17,25},{25,17},{2,10},{10... | collective-permute-start | bytes 393224 | tf_op jit(solution)/shard_map/ppermute | solution.py:32
  89.0 11.8 %all-to-all-start.3 = ((f32[8,32,128]{2,1,0:T(8,128)}), f32[8,32,128]{2,1,0:T(8,128)}, u32[]{:S(2)}, u32[]{:S(2)}) async-start(f32[8,32,128]{2,1,0:T(8,128)} %broadcast_in_dim.14), calls=%async_computation.3 | async-start | bytes 262144 | tf_op jit(solution)/shard_map/all_to_all | solution.py:58
  97.4 29.2 %collective-permute-start.13 = (f32[128,256]{1,0:T(8,128)}, f32[128,256]{1,0:T(8,128)}, u32[]{:S(2)}, u32[]{:S(2)}) collective-permute-start(f32[128,256]{1,0:T(8,128)} %add.294), channel_id=1, source_target_pairs={{0,1},{1,0},{2,3},{3,2},{4,5},{5,4},{6,7},{7,6},{8,9},{9,8},{10,11... | collective-permute-start | bytes 393224 | tf_op jit(solution)/shard_map/ppermute | solution.py:32
  103.9 26.2 %copy-start.16 = (bf16[256,256]{0,1:T(8,128)(2,1)S(1)}, bf16[256,256]{0,1:T(8,128)(2,1)}, u32[]{:S(2)}) copy-start(bf16[256,256]{0,1:T(8,128)(2,1)} %copy-done.15) | copy-start | bytes 393220
  104.2 25.9 %collective-permute-start.17 = (f32[256,128]{1,0:T(8,128)S(1)}, f32[256,128]{1,0:T(8,128)S(1)}, u32[]{:S(2)}, u32[]{:S(2)}) collective-permute-start(f32[256,128]{1,0:T(8,128)S(1)} %get-tuple-element.36), channel_id=1, source_target_pairs={{1,0},{2,1},{3,2},{4,3},{5,4},{6,5},{7,6},{9,8},{10,9},{11,10},{12... | collective-permute-start | bytes 393224 | tf_op jit(solution)/shard_map/ppermute | solution.py:193
  105.5 24.9 %collective-permute-start.18 = (f32[256,128]{1,0:T(8,128)S(1)}, f32[256,128]{1,0:T(8,128)S(1)}, u32[]{:S(2)}, u32[]{:S(2)}) collective-permute-start(f32[256,128]{1,0:T(8,128)S(1)} %get-tuple-element.39), channel_id=1, source_target_pairs={{0,1},{1,2},{2,3},{3,4},{4,5},{5,6},{6,7},{8,9},{9,10},{10,11},{11... | collective-permute-start | bytes 393224 | tf_op jit(solution)/shard_map/ppermute | solution.py:193
  110.1 20.6 %collective-permute-start.19 = (f32[256,128]{1,0:T(8,128)S(1)}, f32[256,128]{1,0:T(8,128)S(1)}, u32[]{:S(2)}, u32[]{:S(2)}) collective-permute-start(f32[256,128]{1,0:T(8,128)S(1)} %get-tuple-element.38), channel_id=1, source_target_pairs={{8,0},{16,8},{24,16},{9,1},{17,9},{25,17},{10,2},{18,10},{26,18},{... | collective-permute-start | bytes 393224 | tf_op jit(solution)/shard_map/ppermute | solution.py:193
  111.4 19.6 %collective-permute-start.20 = (f32[256,128]{1,0:T(8,128)S(1)}, f32[256,128]{1,0:T(8,128)S(1)}, u32[]{:S(2)}, u32[]{:S(2)}) collective-permute-start(f32[256,128]{1,0:T(8,128)S(1)} %get-tuple-element.37), channel_id=1, source_target_pairs={{0,8},{8,16},{16,24},{1,9},{9,17},{17,25},{2,10},{10,18},{18,26},{... | collective-permute-start | bytes 393224 | tf_op jit(solution)/shard_map/ppermute | solution.py:193
  127.6 16.2 %collective-permute-start.14 = (f32[128,256]{1,0:T(8,128)S(1)}, f32[128,256]{1,0:T(8,128)S(1)}, u32[]{:S(2)}, u32[]{:S(2)}) collective-permute-start(f32[128,256]{1,0:T(8,128)S(1)} %add.295), channel_id=1, source_target_pairs={{0,16},{8,24},{16,0},{24,8},{1,17},{9,25},{17,1},{25,9},{2,18},{10... | collective-permute-start | bytes 393224 | tf_op jit(solution)/shard_map/ppermute | solution.py:32
  133.5 12.4 %copy-start.12 = (f32[1024,128]{0,1:T(8,128)}, f32[1024,128]{0,1:T(8,128)S(1)}, u32[]{:S(2)}) copy-start(f32[1024,128]{0,1:T(8,128)S(1)} %slice_add_fusion.3) | copy-start | bytes 1572868
  133.6 11.0 %collective-permute-start.21 = (f32[256,128]{0,1:T(8,128)S(1)}, f32[256,128]{0,1:T(8,128)S(1)}, u32[]{:S(2)}, u32[]{:S(2)}) collective-permute-start(f32[256,128]{0,1:T(8,128)S(1)} %get-tuple-element.32), channel_id=1, source_target_pairs={{1,0},{2,1},{3,2},{4,3},{5,4},{6,5},{7,6},{9,8},{10,9},{11,10},{12... | collective-permute-start | bytes 393224 | tf_op jit(solution)/shard_map/ppermute | solution.py:193
  134.9 9.9 %collective-permute-start.22 = (f32[256,128]{0,1:T(8,128)S(1)}, f32[256,128]{0,1:T(8,128)S(1)}, u32[]{:S(2)}, u32[]{:S(2)}) collective-permute-start(f32[256,128]{0,1:T(8,128)S(1)} %get-tuple-element.35), channel_id=1, source_target_pairs={{0,1},{1,2},{2,3},{3,4},{4,5},{5,6},{6,7},{8,9},{9,10},{10,11},{11... | collective-permute-start | bytes 393224 | tf_op jit(solution)/shard_map/ppermute | solution.py:193
  139.5 6.2 %collective-permute-start.23 = (f32[256,128]{0,1:T(8,128)S(1)}, f32[256,128]{0,1:T(8,128)S(1)}, u32[]{:S(2)}, u32[]{:S(2)}) collective-permute-start(f32[256,128]{0,1:T(8,128)S(1)} %get-tuple-element.34), channel_id=1, source_target_pairs={{8,0},{16,8},{24,16},{9,1},{17,9},{25,17},{10,2},{18,10},{26,18},{... | collective-permute-start | bytes 393224 | tf_op jit(solution)/shard_map/ppermute | solution.py:193
  140.8 5.8 %collective-permute-start.24 = (f32[256,128]{0,1:T(8,128)S(1)}, f32[256,128]{0,1:T(8,128)S(1)}, u32[]{:S(2)}, u32[]{:S(2)}) collective-permute-start(f32[256,128]{0,1:T(8,128)S(1)} %get-tuple-element.33), channel_id=1, source_target_pairs={{0,8},{8,16},{16,24},{1,9},{9,17},{17,25},{2,10},{10,18},{18,26},{... | collective-permute-start | bytes 393224 | tf_op jit(solution)/shard_map/ppermute | solution.py:193
  143.8 5.8 %collective-permute-start.15 = (f32[128,256]{1,0:T(8,128)S(1)}, f32[128,256]{1,0:T(8,128)S(1)}, u32[]{:S(2)}, u32[]{:S(2)}) collective-permute-start(f32[128,256]{1,0:T(8,128)S(1)} %add.296), channel_id=1, source_target_pairs={{0,2},{1,3},{2,0},{3,1},{4,6},{5,7},{6,4},{7,5},{8,10},{9,11},{10,... | collective-permute-start | bytes 393224 | tf_op jit(solution)/shard_map/ppermute | solution.py:32
  149.6 8.7 %collective-permute-start.16 = (f32[128,256]{1,0:T(8,128)S(1)}, f32[128,256]{1,0:T(8,128)S(1)}, u32[]{:S(2)}, u32[]{:S(2)}) collective-permute-start(f32[128,256]{1,0:T(8,128)S(1)} %add.297), channel_id=1, source_target_pairs={{0,4},{1,5},{2,6},{3,7},{4,0},{5,1},{6,2},{7,3},{8,12},{9,13},{10,... | collective-permute-start | bytes 393224 | tf_op jit(solution)/shard_map/ppermute | solution.py:32
  171.1 7.9 %collective-permute-start.25 = (f32[128,256]{1,0:T(8,128)}, f32[128,256]{1,0:T(8,128)}, u32[]{:S(2)}, u32[]{:S(2)}) collective-permute-start(f32[128,256]{1,0:T(8,128)} %fusion.37), channel_id=1, source_target_pairs={{0,8},{8,0},{16,24},{24,16},{1,9},{9,1},{17,25},{25,17},{2,10},{10... | collective-permute-start | bytes 393224 | tf_op jit(solution)/shard_map/ppermute | solution.py:32
  172.0 12.0 %all-to-all-start.4 = ((f32[8,32,128]{2,1,0:T(8,128)}), f32[8,32,128]{2,1,0:T(8,128)}, u32[]{:S(2)}, u32[]{:S(2)}) async-start(f32[8,32,128]{2,1,0:T(8,128)} %broadcast_in_dim.15), calls=%async_computation.4 | async-start | bytes 262144 | tf_op jit(solution)/shard_map/all_to_all | solution.py:58
  180.6 17.0 %collective-permute-start.26 = (f32[128,256]{1,0:T(8,128)}, f32[128,256]{1,0:T(8,128)}, u32[]{:S(2)}, u32[]{:S(2)}) collective-permute-start(f32[128,256]{1,0:T(8,128)} %add.315), channel_id=1, source_target_pairs={{0,1},{1,0},{2,3},{3,2},{4,5},{5,4},{6,7},{7,6},{8,9},{9,8},{10,11... | collective-permute-start | bytes 393224 | tf_op jit(solution)/shard_map/ppermute | solution.py:32
  187.0 12.2 %copy-start.17 = (bf16[256,256]{0,1:T(8,128)(2,1)S(1)}, bf16[256,256]{0,1:T(8,128)(2,1)}, u32[]{:S(2)}) copy-start(bf16[256,256]{0,1:T(8,128)(2,1)} %copy-done.15) | copy-start | bytes 393220
  187.3 13.1 %copy-start.11 = (f32[1024,128]{1,0:T(8,128)}, f32[1024,128]{1,0:T(8,128)S(1)}, u32[]{:S(2)}) copy-start(f32[1024,128]{1,0:T(8,128)S(1)} %fusion.52) | copy-start | bytes 1572868
  187.3 11.9 %collective-permute-start.30 = (f32[256,128]{1,0:T(8,128)S(1)}, f32[256,128]{1,0:T(8,128)S(1)}, u32[]{:S(2)}, u32[]{:S(2)}) collective-permute-start(f32[256,128]{1,0:T(8,128)S(1)} %get-tuple-element.28), channel_id=1, source_target_pairs={{1,0},{2,1},{3,2},{4,3},{5,4},{6,5},{7,6},{9,8},{10,9},{11,10},{12... | collective-permute-start | bytes 393224 | tf_op jit(solution)/shard_map/ppermute | solution.py:193
  188.6 10.9 %collective-permute-start.31 = (f32[256,128]{1,0:T(8,128)S(1)}, f32[256,128]{1,0:T(8,128)S(1)}, u32[]{:S(2)}, u32[]{:S(2)}) collective-permute-start(f32[256,128]{1,0:T(8,128)S(1)} %get-tuple-element.31), channel_id=1, source_target_pairs={{0,1},{1,2},{2,3},{3,4},{4,5},{5,6},{6,7},{8,9},{9,10},{10,11},{11... | collective-permute-start | bytes 393224 | tf_op jit(solution)/shard_map/ppermute | solution.py:193
  193.2 6.6 %collective-permute-start.32 = (f32[256,128]{1,0:T(8,128)S(1)}, f32[256,128]{1,0:T(8,128)S(1)}, u32[]{:S(2)}, u32[]{:S(2)}) collective-permute-start(f32[256,128]{1,0:T(8,128)S(1)} %get-tuple-element.30), channel_id=1, source_target_pairs={{8,0},{16,8},{24,16},{9,1},{17,9},{25,17},{10,2},{18,10},{26,18},{... | collective-permute-start | bytes 393224 | tf_op jit(solution)/shard_map/ppermute | solution.py:193
  194.5 5.6 %collective-permute-start.33 = (f32[256,128]{1,0:T(8,128)S(1)}, f32[256,128]{1,0:T(8,128)S(1)}, u32[]{:S(2)}, u32[]{:S(2)}) collective-permute-start(f32[256,128]{1,0:T(8,128)S(1)} %get-tuple-element.29), channel_id=1, source_target_pairs={{0,8},{8,16},{16,24},{1,9},{9,17},{17,25},{2,10},{10,18},{18,26},{... | collective-permute-start | bytes 393224 | tf_op jit(solution)/shard_map/ppermute | solution.py:193
  199.2 21.4 %collective-permute-start.27 = (f32[128,256]{1,0:T(8,128)}, f32[128,256]{1,0:T(8,128)}, u32[]{:S(2)}, u32[]{:S(2)}) collective-permute-start(f32[128,256]{1,0:T(8,128)} %add.316), channel_id=1, source_target_pairs={{0,16},{8,24},{16,0},{24,8},{1,17},{9,25},{17,1},{25,9},{2,18},{10... | collective-permute-start | bytes 393224 | tf_op jit(solution)/shard_map/ppermute | solution.py:32
  203.9 18.3 %collective-permute-start.34 = (f32[256,128]{0,1:T(8,128)}, f32[256,128]{0,1:T(8,128)}, u32[]{:S(2)}, u32[]{:S(2)}) collective-permute-start(f32[256,128]{0,1:T(8,128)} %get-tuple-element.24), channel_id=1, source_target_pairs={{1,0},{2,1},{3,2},{4,3},{5,4},{6,5},{7,6},{9,8},{10,9},{11,10},{12... | collective-permute-start | bytes 393224 | tf_op jit(solution)/shard_map/ppermute | solution.py:193
  211.3 13.0 %collective-permute-start.35 = (f32[256,128]{0,1:T(8,128)}, f32[256,128]{0,1:T(8,128)S(1)}, u32[]{:S(2)}, u32[]{:S(2)}) collective-permute-start(f32[256,128]{0,1:T(8,128)} %get-tuple-element.27), channel_id=1, source_target_pairs={{0,1},{1,2},{2,3},{3,4},{4,5},{5,6},{6,7},{8,9},{9,10},{10,11},{11... | collective-permute-start | bytes 393224 | tf_op jit(solution)/shard_map/ppermute | solution.py:193
  215.9 9.3 %collective-permute-start.36 = (f32[256,128]{0,1:T(8,128)}, f32[256,128]{0,1:T(8,128)S(1)}, u32[]{:S(2)}, u32[]{:S(2)}) collective-permute-start(f32[256,128]{0,1:T(8,128)} %get-tuple-element.26), channel_id=1, source_target_pairs={{8,0},{16,8},{24,16},{9,1},{17,9},{25,17},{10,2},{18,10},{26,18},{... | collective-permute-start | bytes 393224 | tf_op jit(solution)/shard_map/ppermute | solution.py:193
  217.2 8.9 %collective-permute-start.37 = (f32[256,128]{0,1:T(8,128)}, f32[256,128]{0,1:T(8,128)S(1)}, u32[]{:S(2)}, u32[]{:S(2)}) collective-permute-start(f32[256,128]{0,1:T(8,128)} %get-tuple-element.25), channel_id=1, source_target_pairs={{0,8},{8,16},{16,24},{1,9},{9,17},{17,25},{2,10},{10,18},{18,26},{... | collective-permute-start | bytes 393224 | tf_op jit(solution)/shard_map/ppermute | solution.py:193
  221.6 5.8 %collective-permute-start.28 = (f32[128,256]{1,0:T(8,128)S(1)}, f32[128,256]{1,0:T(8,128)S(1)}, u32[]{:S(2)}, u32[]{:S(2)}) collective-permute-start(f32[128,256]{1,0:T(8,128)S(1)} %add.317), channel_id=1, source_target_pairs={{0,2},{1,3},{2,0},{3,1},{4,6},{5,7},{6,4},{7,5},{8,10},{9,11},{10,... | collective-permute-start | bytes 393224 | tf_op jit(solution)/shard_map/ppermute | solution.py:32
  226.1 19.9 %copy-start.33 = (f32[256,128]{1,0:T(8,128)S(1)}, f32[256,128]{1,0:T(8,128)}, u32[]{:S(2)}) copy-start(f32[256,128]{1,0:T(8,128)} %copy-done.32) | copy-start | bytes 393220
  226.1 19.9 %copy-start.35 = (f32[256,128]{1,0:T(8,128)S(1)}, f32[256,128]{1,0:T(8,128)}, u32[]{:S(2)}) copy-start(f32[256,128]{1,0:T(8,128)} %copy-done.34) | copy-start | bytes 393220
  227.5 10.0 %collective-permute-start.29 = (f32[128,256]{1,0:T(8,128)S(1)}, f32[128,256]{1,0:T(8,128)S(1)}, u32[]{:S(2)}, u32[]{:S(2)}) collective-permute-start(f32[128,256]{1,0:T(8,128)S(1)} %add.318), channel_id=1, source_target_pairs={{0,4},{1,5},{2,6},{3,7},{4,0},{5,1},{6,2},{7,3},{8,12},{9,13},{10,... | collective-permute-start | bytes 393224 | tf_op jit(solution)/shard_map/ppermute | solution.py:32
  250.6 14.1 %copy-start.24 = (f32[1024,128]{1,0:T(8,128)}, f32[1024,128]{1,0:T(8,128)S(1)}, u32[]{:S(2)}) copy-start(f32[1024,128]{1,0:T(8,128)S(1)} %convolution_subtract_fusion.1) | copy-start | bytes 1572868
  251.2 13.6 %copy-start.25 = (f32[1024,128]{1,0:T(8,128)}, f32[1024,128]{1,0:T(8,128)S(1)}, u32[]{:S(2)}) copy-start(f32[1024,128]{1,0:T(8,128)S(1)} %convolution_subtract_fusion.3) | copy-start | bytes 1572868
  252.4 1.4 collective-permute-start.38
  253.9 5.7 %collective-permute-start.39 = (f32[128,256]{1,0:T(8,128)S(1)}, f32[128,256]{1,0:T(8,128)S(1)}, u32[]{:S(2)}, u32[]{:S(2)}) collective-permute-start(f32[128,256]{1,0:T(8,128)S(1)} %add.341), channel_id=1, source_target_pairs={{0,1},{1,0},{2,3},{3,2},{4,5},{5,4},{6,7},{7,6},{8,9},{9,8},{10,11... | collective-permute-start | bytes 393224 | tf_op jit(solution)/shard_map/ppermute | solution.py:32
  259.6 5.0 %collective-permute-start.40 = (f32[128,256]{1,0:T(8,128)S(1)}, f32[128,256]{1,0:T(8,128)S(1)}, u32[]{:S(2)}, u32[]{:S(2)}) collective-permute-start(f32[128,256]{1,0:T(8,128)S(1)} %add.342), channel_id=1, source_target_pairs={{0,16},{8,24},{16,0},{24,8},{1,17},{9,25},{17,1},{25,9},{2,18},{10... | collective-permute-start | bytes 393224 | tf_op jit(solution)/shard_map/ppermute | solution.py:32
  264.7 19.9 %copy-start.19 = (f32[1024,128]{1,0:T(8,128)S(1)}, f32[1024,128]{1,0:T(8,128)}, u32[]{:S(2)}) copy-start(f32[1024,128]{1,0:T(8,128)} %copy-done.18) | copy-start | bytes 1572868
  264.7 7.1 %collective-permute-start.41 = (f32[128,256]{1,0:T(8,128)S(1)}, f32[128,256]{1,0:T(8,128)S(1)}, u32[]{:S(2)}, u32[]{:S(2)}) collective-permute-start(f32[128,256]{1,0:T(8,128)S(1)} %add.343), channel_id=1, source_target_pairs={{0,2},{1,3},{2,0},{3,1},{4,6},{5,7},{6,4},{7,5},{8,10},{9,11},{10,... | collective-permute-start | bytes 393224 | tf_op jit(solution)/shard_map/ppermute | solution.py:32
  271.8 6.1 %collective-permute-start.42 = (f32[128,256]{1,0:T(8,128)S(1)}, f32[128,256]{1,0:T(8,128)S(1)}, u32[]{:S(2)}, u32[]{:S(2)}) collective-permute-start(f32[128,256]{1,0:T(8,128)S(1)} %add.344), channel_id=1, source_target_pairs={{0,4},{1,5},{2,6},{3,7},{4,0},{5,1},{6,2},{7,3},{8,12},{9,13},{10,... | collective-permute-start | bytes 393224 | tf_op jit(solution)/shard_map/ppermute | solution.py:32
  (51 other events, 129.2 us)
where the time goes:
time: 297 us; the launch traced here: 292 us
  starting transfers between devices  130 us (44%)
  matrix products  51.8 us (17%)
  waiting for transfers between devices  37.5 us (13%)
  Pallas kernels  28.7 us (10%)
  other arithmetic  27.3 us (9%)
  local copies, waits for them, and re-layouts  13.9 us (5%)
  between operations  3.07 us (1%)
    ppermute x28, starting transfers between devices, assemble(): lax.ppermute(block[(d ^ 1) * zone:((d ^ 1) + 1) * zone], axis, line(axis,...  85.5 us
    pallas_call x5, Pallas kernels, small(): pl.pallas_call(kernel, out_shape=[square] * count, name=name, cost_estima...  28.7 us
    ppermute x15, waiting for transfers between devices, swap(): lax.ppermute(x, axis, [(i, i ^ bit) for i in range(lax.axis_size(axis))])  26.8 us
    dot_general x16, matrix products, mix(): return jnp.dot(block, mixing, precision=HIGHEST)  21.8 us
    ppermute x15, starting transfers between devices, swap(): lax.ppermute(x, axis, [(i, i ^ bit) for i in range(lax.axis_size(axis))])  20.5 us
    dot_general x40, matrix products, times(): both = jnp.dot(matrix, halves(x), preferred_element_type=jnp.float32)  19.6 us
    all_to_all x4, starting transfers between devices, gather_sub(): out = lax.all_to_all(copies, 'sub', 0, 0)  17.8 us
    add x15, other arithmetic, total(): x = x + swap(x, axis, bit)  9.01 us
  transfers between devices with their start and end apart: 48, of which 15 were waited for; matrix products, arithmetic and copies ran while one was open for 19% of the time, Pallas kernels for 4%

commit v1 on v0

v1 whole, which is shorter than its diff:
```python
import jax
import jax.numpy as jnp
from jax import lax
from jax.experimental import pallas as pl
from jax.experimental.pallas import tpu as pltpu
from jax.sharding import PartitionSpec as P

ITERS = 3
HIGHEST = lax.Precision.HIGHEST


def swap(x, axis, bit):
    return lax.ppermute(x, axis, [(i, i ^ bit) for i in range(lax.axis_size(axis))])


def bits_of(axis):
    count = lax.axis_size(axis)
    if count & (count - 1):
        raise ValueError("axis size")
    return [1 << b for b in range(count.bit_length() - 1)]


def total(x):
    group_bits, sub_bits = bits_of("group"), bits_of("sub")
    order = []
    for i in range(max(len(group_bits), len(sub_bits))):
        if i < len(group_bits):
            order.append(("group", group_bits[i]))
        if i < len(sub_bits):
            order.append(("sub", sub_bits[i]))
    for axis, bit in order:
        x = x + swap(x, axis, bit)
    return x


def gather_sub(x):
    count = lax.axis_size("sub")
    copies = jnp.broadcast_to(x[None], (count,) + x.shape)
    out = lax.all_to_all(copies, "sub", 0, 0)
    return out.reshape((-1,) + x.shape[1:])


def one_hot(rows, count):
    return rows[:, None] == jnp.arange(count, dtype=jnp.int32)[None, :]


def selected_inverse(coarse_map, inverse_rows):
    modes = coarse_map.shape[0]
    rows_here, coarse_total = inverse_rows.shape
    maps = gather_sub(coarse_map)
    count = maps.shape[0] // modes
    columns = one_hot(maps, coarse_total).astype(jnp.bfloat16)
    picked_columns = lax.dot_general(
        inverse_rows, columns, (((1,), (1,)), ((), ())), preferred_element_type=jnp.float32
    ).astype(jnp.bfloat16)
    first = lax.axis_index("sub") * rows_here
    rows = one_hot(maps - first, rows_here).astype(jnp.bfloat16)
    table = jnp.dot(rows, picked_columns, preferred_element_type=jnp.float32).astype(jnp.bfloat16)
    table = table.reshape(count, modes, count * modes)
    return lax.all_to_all(table, "sub", 0, 0).sum(axis=0)


def eliminate(matrix, block, tile=8):
    n, width = matrix.shape[0], block.shape[1]
    sublane = lax.broadcasted_iota(jnp.int32, (tile, 1), 0)
    left = [matrix[i : i + tile] for i in range(0, n, tile)]
    right = [block[i : i + tile] for i in range(0, n, tile)]
    for k in range(n // tile):
        pivot_left, pivot_right = left[k], right[k]
        at = k * tile
        spread = [
            jnp.broadcast_to(pivot_left[:, at + j : at + j + 1], (tile, n)) for j in range(tile)
        ]
        for j in range(tile):
            inverse = 1.0 / spread[j][j : j + 1]
            here = sublane == j
            column = spread[j]

            def cleared(rows, column=column, inverse=inverse, here=here, j=j):
                pivot = rows[j : j + 1] * inverse
                return jnp.where(here, pivot, rows - column * pivot)

            for i in range(j + 1, tile):
                spread[i] = cleared(spread[i])
            pivot_left, pivot_right = cleared(pivot_left), cleared(pivot_right)
        for i in range(n // tile):
            if i == k:
                continue
            old = left[i]
            new_left, new_right = old, right[i]
            for j in range(tile):
                scale = jnp.broadcast_to(old[:, at + j : at + j + 1], (tile, n))
                new_left = new_left - scale * pivot_left[j : j + 1]
                new_right = new_right - scale * pivot_right[j : j + 1]
            left[i], right[i] = new_left, new_right
        left[k], right[k] = pivot_left, pivot_right
    return jnp.concatenate(right, axis=0)


def exact(a, b):
    return jnp.dot(a, b, precision=HIGHEST, preferred_element_type=jnp.float32)


def symmetric(a):
    return (a + a.T) * 0.5


def halves(x):
    high = x.astype(jnp.bfloat16)
    low = (x - high.astype(jnp.float32)).astype(jnp.bfloat16)
    return jnp.concatenate([high, low], axis=1)


def folded(both):
    n = both.shape[1] // 2
    return both[:, :n] + both[:, n:]


def times(matrix, x, contracting=1):
    dims = (((contracting,), (0,)), ((), ()))
    if x.dtype == jnp.bfloat16:
        return lax.dot_general(matrix, x, dims, preferred_element_type=jnp.float32)
    return folded(lax.dot_general(matrix, halves(x), dims, preferred_element_type=jnp.float32))


def mixer(mixing):
    both = halves(mixing)
    return jnp.concatenate([both, both], axis=0)


def mix(block, mixer_value):
    return folded(jnp.dot(halves(block), mixer_value, preferred_element_type=jnp.float32))


def local_gram(weighted, right):
    n = weighted.shape[1]
    both = lax.dot_general(
        halves(weighted),
        halves(right),
        (((0,), (0,)), ((), ())),
        preferred_element_type=jnp.float32,
    )
    both = both[:n] + both[n:]
    return both[:, :n] + both[:, n:]


def zone_of(parity, slot):
    flip = parity[slot // 2]
    return 2 * (slot // 2) + (flip if slot % 2 == 0 else 1 - flip)


def assemble_into(parity, tables, slots, received, out):
    zone = slots[0].shape[0]
    for slot in range(4):
        start = pl.multiple_of(zone_of(parity, slot) * zone, zone)
        value = slots[slot][...].astype(jnp.float32) + times(tables[slot], received[slot][...])
        out[pl.ds(start, zone)] = value


def slots_from(parity, block, slots):
    zone = slots[0].shape[0]
    for slot in range(4):
        pair = 2 * (slot // 2)
        swapped = parity[slot // 2] == (1 if slot % 2 == 0 else 0)
        low, high = block[pair * zone : (pair + 1) * zone], block[(pair + 1) * zone : (pair + 2) * zone]
        slots[slot][...] = jnp.where(swapped, high, low)


def coarse_pieces(basis, scaled, pieces):
    piece = times(basis[...], scaled)
    for i in range(pieces.shape[0]):
        pieces[i] = piece


def tables_kernel(parity, rows, counts, tables, weight):
    capacity = rows.shape[2]
    place = lax.broadcasted_iota(jnp.int32, (capacity, capacity), 0)
    entry = lax.broadcasted_iota(jnp.int32, (1, capacity), 1)
    for slot in range(4):
        d = zone_of(parity, slot)
        partner_zone = zone_of(parity, slot ^ 1)
        own = rows[0, pl.ds(d, 1)] - d * capacity
        partner = rows[1, pl.ds(d, 1)] - partner_zone * capacity
        own = jnp.where(entry < counts[d], own, -1)
        to = (place == own).astype(jnp.float32).astype(jnp.bfloat16)
        source = (place == partner).astype(jnp.float32).astype(jnp.bfloat16)
        table = lax.dot_general(
            to, source, (((1,), (1,)), ((), ())), preferred_element_type=jnp.float32
        )
        tables[slot] = table.astype(jnp.bfloat16)
        ones = jnp.ones((capacity, weight.shape[1]), jnp.bfloat16)
        shared = jnp.dot(table.astype(jnp.bfloat16), ones, preferred_element_type=jnp.float32)
        weight[pl.ds(pl.multiple_of(d * capacity, capacity), capacity)] = 1.0 / (1.0 + shared)


def start_kernel(parity, tables, weight, basis, *refs):
    slots, received, (block, pieces) = refs[:4], refs[4:8], refs[8:]
    assemble_into(parity, tables, slots, received, block)
    coarse_pieces(basis, weight[...] * block[...], pieces)


def gram_start_kernel(parity, tables, weight, basis, z, r, *refs):
    slots, received, (block, pieces, grams) = refs[:4], refs[4:8], refs[8:]
    n = z.shape[1]
    assemble_into(parity, tables, slots, received, block)
    coarse_pieces(basis, weight[...] * block[...], pieces)
    weighted = weight[...] * z[...]
    grams[:, :n] = local_gram(weighted, r[...])
    grams[:, n:] = local_gram(weighted, block[...])


def local_kernel(weight, matrix, block, out):
    out[...] = times(matrix[...], weight[...] * block[...])


def finish_kernel(parity, weight, basis, chosen, pieces, local, *slots):
    count, modes, n = pieces.shape
    picked = times(chosen[...], pieces[...].reshape(count * modes, n))
    smoothed = weight[...] * (local[...] + times(basis[...], picked, contracting=0))
    slots_from(parity, smoothed, slots)


def operator_kernel(parity, tables, matrix, *refs):
    slots, received, (block, out) = refs[:4], refs[4:8], (refs[8], refs[9:])
    assemble_into(parity, tables, slots, received, block)
    slots_from(parity, times(matrix[...], block[...]), out)


def first_update_kernel(parity, tables, weight, basis, grams, z, w, r, m, *refs):
    slots, received = refs[:4], refs[4:8]
    x, r_out, z_out, w_out, image, grams_out, pieces = refs[8:]
    n = z.shape[1]
    assemble_into(parity, tables, slots, received, image)
    alpha = mixer(eliminate(symmetric(grams[:, n:]), grams[:, :n]))
    w_new = w[...] - mix(image[...], alpha)
    w_out[...] = w_new
    coarse_pieces(basis, weight[...] * w_new, pieces)
    x[...] = mix(z[...], alpha)
    r_new = r[...] - mix(w[...], alpha)
    r_out[...] = r_new
    z_new = z[...] - mix(m[...], alpha)
    z_out[...] = z_new
    weighted = weight[...] * z_new
    grams_out[:, :n] = local_gram(weighted, r_new)
    grams_out[:, n:] = local_gram(weighted, w_new)


def step_sizes(grams, inner_inverse, curvature):
    n = grams.shape[0]
    beta = exact(inner_inverse[...], grams[:, :n])
    bent = grams[:, n:] - exact(beta.T, exact(curvature[...], beta))
    return beta, bent, eliminate(symmetric(bent), grams[:, :n])


def next_update_kernel(
    parity, tables, weight, basis, grams, inner_inverse, curvature, z, w, r, m, p, s, q, t, x, *refs
):
    slots, received = refs[:4], refs[4:8]
    (
        x_out, r_out, z_out, w_out, p_out, s_out, q_out, t_out, curvature_out, grams_out, pieces
    ) = refs[8:]
    n = z.shape[1]
    assemble_into(parity, tables, slots, received, t_out)
    beta, bent, alpha = step_sizes(grams, inner_inverse, curvature)
    curvature_out[...] = bent
    beta, alpha = mixer(beta), mixer(alpha)
    t_out[...] = t_out[...] + mix(t[...], beta)
    w_new = w[...] - mix(t_out[...], alpha)
    w_out[...] = w_new
    coarse_pieces(basis, weight[...] * w_new, pieces)
    p_out[...] = z[...] + mix(p[...], beta)
    s_out[...] = w[...] + mix(s[...], beta)
    q_out[...] = m[...] + mix(q[...], beta)
    x_out[...] = x[...] + mix(p_out[...], alpha)
    r_new = r[...] - mix(s_out[...], alpha)
    r_out[...] = r_new
    z_new = z[...] - mix(q_out[...], alpha)
    z_out[...] = z_new
    weighted = weight[...] * z_new
    grams_out[:, :n] = local_gram(weighted, r_new)
    grams_out[:, n:] = local_gram(weighted, w_new)


def last_update_kernel(grams, inner_inverse, curvature, z, w, r, p, s, x, x_out, r_out):
    beta, _, alpha = step_sizes(grams, inner_inverse, curvature)
    beta, alpha = mixer(beta), mixer(alpha)
    x_out[...] = x[...] + mix(z[...] + mix(p[...], beta), alpha)
    r_out[...] = r[...] - mix(w[...] + mix(s[...], beta), alpha)


def inverse_kernel(grams, out):
    n = out.shape[0]
    rows = lax.broadcasted_iota(jnp.int32, (n, n), 0)
    columns = lax.broadcasted_iota(jnp.int32, (n, n), 1)
    out[...] = eliminate(symmetric(grams[:, :n]), (rows == columns).astype(jnp.float32))


VMEM = pl.BlockSpec(memory_space=pltpu.VMEM)
SMEM = pl.BlockSpec(memory_space=pltpu.SMEM)


def call(kernel, name, flops, outs, *args):
    shapes = [jax.ShapeDtypeStruct(shape, dtype) for shape, dtype in outs]
    moved = sum(a.size * a.dtype.itemsize for a in (*args, *shapes))
    return pl.pallas_call(
        kernel,
        out_shape=shapes,
        in_specs=[SMEM if a.ndim == 1 else VMEM for a in args],
        out_specs=[VMEM] * len(shapes),
        name=name,
        compiler_params=pltpu.CompilerParams(vmem_limit_bytes=32 * 1024 * 1024),
        cost_estimate=pl.CostEstimate(flops=flops, bytes_accessed=moved, transcendentals=0),
    )(*args)


def pairs(axis, first):
    count = lax.axis_size(axis)
    low = range(first, count - 1, 2)
    return [(i, i + 1) for i in low] + [(i + 1, i) for i in low]


def exchange(slots):
    return [
        lax.ppermute(slot, axis, pairs(axis, first))
        for slot, (axis, first) in zip(
            slots, (("sub", 0), ("sub", 1), ("group", 0), ("group", 1))
        )
    ]


def shards(
    schur, local_inverse, rhs_parts, basis, coarse_map, coarse_inverse, shared_rows, shared_counts
):
    schur, local_inverse, basis = schur[0, 0], local_inverse[0, 0], basis[0, 0]
    rhs = rhs_parts[0, 0]
    rows, columns = rhs.shape
    zone = shared_rows.shape[-1]
    modes = basis.shape[0]
    subs = lax.axis_size("sub")
    parity = jnp.stack([lax.axis_index("sub") % 2, lax.axis_index("group") % 2]).astype(jnp.int32)
    block = ((rows, columns), jnp.float32)
    part = ((zone, columns), jnp.float32)
    square = ((columns, columns), jnp.float32)
    double = ((columns, 2 * columns), jnp.float32)
    shares = ((subs, modes, columns), jnp.float32)
    solve_flops = 400_000_000
    product_flops = 4 * rows * rows * columns

    def rhs_zone(slot):
        return lax.dynamic_slice_in_dim(rhs, zone_of(parity, slot) * zone, zone, axis=0)

    rhs_slots = [rhs_zone(slot) for slot in range(4)]
    received = exchange(rhs_slots)
    tables, weight = call(
        tables_kernel,
        "shared_row_tables",
        16 * zone**3,
        [((4, zone, zone), jnp.bfloat16), block],
        parity,
        shared_rows[0, 0],
        shared_counts[0, 0],
    )
    chosen = selected_inverse(coarse_map[0, 0], coarse_inverse[0])

    def precondition(vector, pieces):
        gathered = lax.all_to_all(pieces, "sub", 0, 0)
        (local,) = call(
            local_kernel, "local_inverse", product_flops, [block], weight, local_inverse, vector
        )
        slots = call(
            finish_kernel,
            "coarse_part",
            product_flops // 8,
            [part] * 4,
            parity,
            weight,
            basis,
            chosen,
            gathered,
            local,
        )
        return slots, exchange(slots)

    def operator(slots, received):
        vector, *image = call(
            operator_kernel,
            "operator",
            product_flops,
            [block] + [part] * 4,
            parity,
            tables,
            schur,
            *slots,
            *received,
        )
        return vector, image, exchange(image)

    r, pieces = call(
        start_kernel,
        "start",
        product_flops // 8,
        [block, shares],
        parity,
        tables,
        weight,
        basis,
        *rhs_slots,
        *received,
    )
    z, image, received = operator(*precondition(r, pieces))
    w, pieces, local = call(
        gram_start_kernel,
        "start_grams",
        product_flops // 4,
        [block, shares, double],
        parity,
        tables,
        weight,
        basis,
        z,
        r,
        *image,
        *received,
    )
    for iteration in range(ITERS):
        grams = total(local)
        if iteration + 1 == ITERS:
            break
        (inverse,) = call(inverse_kernel, "inner_inverse", solve_flops, [square], grams)
        m, image, received = operator(*precondition(w, pieces))
        common = (parity, tables, weight, basis, grams)
        if iteration == 0:
            p, s, q, curvature = z, w, m, grams[:, columns:]
            x, r, z, w, t, local, pieces = call(
                first_update_kernel,
                "first_update",
                2 * solve_flops,
                [block] * 5 + [double, shares],
                *common,
                z,
                w,
                r,
                m,
                *image,
                *received,
            )
        else:
            x, r, z, w, p, s, q, t, curvature, local, pieces = call(
                next_update_kernel,
                "next_update",
                2 * solve_flops,
                [block] * 8 + [square, double, shares],
                *common,
                inner_inverse,
                curvature,
                z,
                w,
                r,
                m,
                p,
                s,
                q,
                t,
                x,
                *image,
                *received,
            )
        inner_inverse = inverse
    x, r = call(
        last_update_kernel,
        "last_update",
        2 * solve_flops,
        [block, block],
        grams,
        inner_inverse,
        curvature,
        z,
        w,
        r,
        p,
        s,
        x,
    )
    return x[None, None], r[None, None]


def solution(mesh):
    placed = (
        P("group", "sub", None, None),
        P("group", "sub", None, None),
        P("group", "sub", None, None),
        P("group", "sub", None, None),
        P("group", "sub", None),
        P("group", "sub", None),
        P("group", "sub", None, None, None),
        P("group", "sub", None),
    )
    return jax.shard_map(
        shards,
        mesh=mesh,
        in_specs=placed,
        out_specs=(P("group", "sub", None, None), P("group", "sub", None, None)),
        check_vma=False,
    )
```

time: 297 us -> 219 us (0.74); the launches traced: 292 us -> 217 us
  matrix products: 51.8 us -> 1.23 us
  starting transfers between devices: 130 us -> 98.3 us
  other arithmetic: 27.3 us -> 7.14 us
  Pallas kernels: 28.7 us -> 43.5 us
  local copies, waits for them, and re-layouts: 13.9 us -> 25.2 us
  waiting for transfers between devices: 37.5 us -> 40.5 us
    ppermute x28, starting transfers between devices: 85.5 us -> 33.2 us  [exchange(): lax.ppermute(slot, axis, pairs(axis, first))]
    dot_general x66 -> x0, matrix products: 50.5 us -> none  [the longest x16 21.8 us: mix(): return jnp.dot(block, mixing, precision=HIGHEST)]
    all_to_all x0 -> x3, starting transfers between devices: none -> 19.3 us  [precondition(): gathered = lax.all_to_all(pieces, 'sub', 0, 0)]
    unnamed x134 -> x86, local copies, waits for them, and re-layouts: 6.21 us -> 22.3 us
    pallas_call x5 -> x17, Pallas kernels: 28.7 us -> 43.5 us  [call(): pl.pallas_call(kernel, out_shape=shapes, in_specs=[SMEM if a.ndim == 1 el...]
    ppermute x15, starting transfers between devices: 20.5 us -> 34.6 us  [swap(): lax.ppermute(x, axis, [(i, i ^ bit) for i in range(lax.axis_size(axis))])]
    all_to_all x4 -> x1, starting transfers between devices: 17.8 us -> 7.28 us  [gather_sub(): out = lax.all_to_all(copies, 'sub', 0, 0)]
    another operation x43 -> x1, other arithmetic: 6.75 us -> 0.08 us  [shards(): jnp.stack([lax.axis_index('sub') % 2, lax.axis_index('group') % 2])]
  transfers between devices with their start and end apart: 48 -> 48, of which waited for: 15 -> 11; matrix products, arithmetic and copies ran while one was open for 19% -> 3% of each run, Pallas kernels for 4% -> 9%
where the time goes in v1:
time: 219 us; the launch traced here: 217 us
  starting transfers between devices  98.3 us (45%)
  Pallas kernels  43.5 us (20%)
  waiting for transfers between devices  40.5 us (18%)
  local copies, waits for them, and re-layouts  25.2 us (12%)
  other arithmetic  7.14 us (3%)
    pallas_call x17, Pallas kernels, call(): pl.pallas_call(kernel, out_shape=shapes, in_specs=[SMEM if a.ndim == 1 el...  43.5 us
    ppermute x15, starting transfers between devices, swap(): lax.ppermute(x, axis, [(i, i ^ bit) for i in range(lax.axis_size(axis))])  34.6 us
    ppermute x28, starting transfers between devices, exchange(): lax.ppermute(slot, axis, pairs(axis, first))  33.2 us
    ppermute x15, waiting for transfers between devices, swap(): lax.ppermute(x, axis, [(i, i ^ bit) for i in range(lax.axis_size(axis))])  24.3 us
    unnamed x86, local copies, waits for them, and re-layouts  22.3 us
    all_to_all x3, starting transfers between devices, precondition(): gathered = lax.all_to_all(pieces, 'sub', 0, 0)  19.3 us
    all_to_all x1, starting transfers between devices, gather_sub(): out = lax.all_to_all(copies, 'sub', 0, 0)  7.28 us
    all_to_all x1, waiting for transfers between devices, gather_sub(): out = lax.all_to_all(copies, 'sub', 0, 0)  6.39 us
  transfers between devices with their start and end apart: 48, of which 11 were waited for; matrix products, arithmetic and copies ran while one was open for 3% of the time, Pallas kernels for 9%

profile of v1, /device:TPU:0, one launch (start us, length us, event | category | flops | bytes accessed | tf_op | source)
XLA Modules:
  0.0 217.3 jit_solution(10316678456061257407)
XLA Ops:
  0.7 1.3 broadcast_in_dim.6
  1.9 7.3 %all-to-all-start = ((s32[8,1,32]{2,1,0:T(1,128)}), s32[8,1,32]{2,1,0:T(1,128)S(1)}, u32[]{:S(2)}, u32[]{:S(2)}) async-start(s32[8,1,32]{2,1,0:T(1,128)} %broadcast_in_dim.6), calls=%async_computation | async-start | bytes 8192 | tf_op jit(solution)/shard_map/all_to_all | solution.py:39
  9.2 6.4 %all-to-all-done = s32[8,1,32]{2,1,0:T(1,128)S(1)} async-done(((s32[8,1,32]{2,1,0:T(1,128)}), s32[8,1,32]{2,1,0:T(1,128)S(1)}, u32[]{:S(2)}, u32[]{:S(2)}) %all-to-all-start) | async-done | bytes 1056 | tf_op jit(solution)/shard_map/all_to_all | solution.py:39
  16.9 1.2 convolution_convert_fusion
  18.1 4.0 %all-to-all-start.1 = ((bf16[8,32,256]{2,1,0:T(8,128)(2,1)}), bf16[8,32,256]{2,1,0:T(8,128)(2,1)}, u32[]{:S(2)}, u32[]{:S(2)}) async-start(bf16[8,32,256]{2,1,0:T(8,128)(2,1)} %bitcast.8), calls=%async_computation.1 | async-start | bytes 262144 | tf_op jit(solution)/shard_map/all_to_all | solution.py:60
  23.1 1.9 collective-permute-start
  27.9 1.2 shared_row_tables.1
  29.2 1.1 start.1
  31.8 7.5 %all-to-all-start.2 = ((f32[8,32,128]{2,1,0:T(8,128)}), f32[8,32,128]{2,1,0:T(8,128)}, u32[]{:S(2)}, u32[]{:S(2)}) async-start(f32[8,32,128]{2,1,0:T(8,128)} %copy-done.40), calls=%async_computation.2 | async-start | bytes 262144 | tf_op jit(solution)/shard_map/all_to_all | solution.py:366
  39.3 1.0 copy-done.13
  42.8 4.0 %all-to-all-done.2.pieces = f32[8,32,128]{2,1,0:T(8,128)} async-done(((f32[8,32,128]{2,1,0:T(8,128)}), f32[8,32,128]{2,1,0:T(8,128)}, u32[]{:S(2)}, u32[]{:S(2)}) %all-to-all-start.2) | async-done | bytes 131104 | tf_op jit(solution)/shard_map/all_to_all | solution.py:366
  46.7 1.0 copy-done.23
  47.8 1.4 coarse_part.3
  50.1 1.1 collective-permute-start.6
  51.9 3.5 %collective-permute-done.4.refs_4_ = f32[256,128]{1,0:T(8,128)S(1)} collective-permute-done((f32[256,128]{1,0:T(8,128)S(1)}, f32[256,128]{1,0:T(8,128)S(1)}, u32[]{:S(2)}, u32[]{:S(2)}) %collective-permute-start.4) | collective-permute-done | bytes 131104 | tf_op jit(solution)/shard_map/ppermute | solution.py:324
  55.4 1.6 copy-done.2
  57.0 1.6 operator.3
  58.6 3.0 %collective-permute-start.10 = (f32[256,128]{1,0:T(8,128)S(1)}, f32[256,128]{1,0:T(8,128)S(1)}, u32[]{:S(2)}, u32[]{:S(2)}) collective-permute-start(f32[256,128]{1,0:T(8,128)S(1)} %get-tuple-element.64.refs_2_), channel_id=1, source_target_pairs={{0,8},{16,24},{8,0},{24,16},{1,9},{17,25},{9,1},{25,17},{2,10},{18... | collective-permute-start | bytes 393224 | tf_op jit(solution)/shard_map/ppermute | solution.py:324
  62.3 3.9 %collective-permute-start.8 = (f32[256,128]{1,0:T(8,128)S(1)}, f32[256,128]{1,0:T(8,128)S(1)}, u32[]{:S(2)}, u32[]{:S(2)}) collective-permute-start(f32[256,128]{1,0:T(8,128)S(1)} %get-tuple-element.62.refs_0_), channel_id=1, source_target_pairs={{0,1},{2,3},{4,5},{6,7},{1,0},{3,2},{5,4},{7,6},{8,9},{10,11},{12,... | collective-permute-start | bytes 393224 | tf_op jit(solution)/shard_map/ppermute | solution.py:324
  66.8 2.3 %collective-permute-done.8.refs_4_ = f32[256,128]{1,0:T(8,128)S(1)} collective-permute-done((f32[256,128]{1,0:T(8,128)S(1)}, f32[256,128]{1,0:T(8,128)S(1)}, u32[]{:S(2)}, u32[]{:S(2)}) %collective-permute-start.8) | collective-permute-done | bytes 131104 | tf_op jit(solution)/shard_map/ppermute | solution.py:324
  69.1 2.1 start_grams.1
  72.6 3.1 %collective-permute-start.12 = (f32[128,256]{1,0:T(8,128)}, f32[128,256]{1,0:T(8,128)}, u32[]{:S(2)}, u32[]{:S(2)}) collective-permute-start(f32[128,256]{1,0:T(8,128)} %get-tuple-element.66), channel_id=1, source_target_pairs={{0,8},{8,0},{16,24},{24,16},{1,9},{9,1},{17,25},{25,17},{2,10},{10... | collective-permute-start | bytes 393224 | tf_op jit(solution)/shard_map/ppermute | solution.py:13
  75.7 6.7 %all-to-all-start.3 = ((f32[8,32,128]{2,1,0:T(8,128)}), f32[8,32,128]{2,1,0:T(8,128)}, u32[]{:S(2)}, u32[]{:S(2)}) async-start(f32[8,32,128]{2,1,0:T(8,128)} %copy-done.39), calls=%async_computation.3 | async-start | bytes 262144 | tf_op jit(solution)/shard_map/all_to_all | solution.py:366
  83.5 2.1 collective-permute-start.13
  85.5 4.2 %collective-permute-done.13 = f32[128,256]{1,0:T(8,128)S(1)} collective-permute-done((f32[128,256]{1,0:T(8,128)S(1)}, f32[128,256]{1,0:T(8,128)S(1)}, u32[]{:S(2)}, u32[]{:S(2)}) %collective-permute-start.13) | collective-permute-done | bytes 131104 | tf_op jit(solution)/shard_map/ppermute | solution.py:13
  90.4 1.9 collective-permute-start.14
  92.3 1.0 copy-done.6
  94.8 1.0 copy-done.27
  95.9 1.4 coarse_part.4
  97.3 1.4 collective-permute-start.17
  101.1 3.5 %collective-permute-start.15 = (f32[128,256]{1,0:T(8,128)S(1)}, f32[128,256]{1,0:T(8,128)S(1)}, u32[]{:S(2)}, u32[]{:S(2)}) collective-permute-start(f32[128,256]{1,0:T(8,128)S(1)} %add.81), channel_id=1, source_target_pairs={{0,2},{1,3},{2,0},{3,1},{4,6},{5,7},{6,4},{7,5},{8,10},{9,11},{10,... | collective-permute-start | bytes 393224 | tf_op jit(solution)/shard_map/ppermute | solution.py:13
  104.6 1.6 copy-done.3
  106.2 1.6 operator.4
  107.7 2.6 %collective-permute-start.21 = (f32[256,128]{1,0:T(8,128)S(1)}, f32[256,128]{1,0:T(8,128)S(1)}, u32[]{:S(2)}, u32[]{:S(2)}) collective-permute-start(f32[256,128]{1,0:T(8,128)S(1)} %get-tuple-element.74.refs_0_), channel_id=1, source_target_pairs={{0,1},{2,3},{4,5},{6,7},{1,0},{3,2},{5,4},{7,6},{8,9},{10,11},{12,... | collective-permute-start | bytes 393224 | tf_op jit(solution)/shard_map/ppermute | solution.py:324
  110.4 2.3 %collective-permute-start.16 = (f32[128,256]{1,0:T(8,128)S(1)}, f32[128,256]{1,0:T(8,128)S(1)}, u32[]{:S(2)}, u32[]{:S(2)}) collective-permute-start(f32[128,256]{1,0:T(8,128)S(1)} %add.82), channel_id=1, source_target_pairs={{0,4},{1,5},{2,6},{3,7},{4,0},{5,1},{6,2},{7,3},{8,12},{9,13},{10,... | collective-permute-start | bytes 393224 | tf_op jit(solution)/shard_map/ppermute | solution.py:13
  113.3 2.6 %collective-permute-start.23 = (f32[256,128]{1,0:T(8,128)S(1)}, f32[256,128]{1,0:T(8,128)S(1)}, u32[]{:S(2)}, u32[]{:S(2)}) collective-permute-start(f32[256,128]{1,0:T(8,128)S(1)} %get-tuple-element.76.refs_2_), channel_id=1, source_target_pairs={{0,8},{16,24},{8,0},{24,16},{1,9},{17,25},{9,1},{25,17},{2,10},{18... | collective-permute-start | bytes 393224 | tf_op jit(solution)/shard_map/ppermute | solution.py:324
  116.8 2.7 %collective-permute-done.16 = f32[128,256]{1,0:T(8,128)S(1)} collective-permute-done((f32[128,256]{1,0:T(8,128)S(1)}, f32[128,256]{1,0:T(8,128)S(1)}, u32[]{:S(2)}, u32[]{:S(2)}) %collective-permute-start.16) | collective-permute-done | bytes 131104 | tf_op jit(solution)/shard_map/ppermute | solution.py:13
  119.6 7.1 %first_update.1 = (f32[1024,128]{1,0:T(8,128)S(1)}, f32[1024,128]{1,0:T(8,128)S(1)}, f32[1024,128]{1,0:T(8,128)S(1)}, f32[1024,128]{1,0:T(8,128)S(1)}, f32[1024,...) custom-call(s32[2]{0:T(128)S(1)} %pad_add_fusion.parity, ...), custom_call_target="tpu_custom_call" | custom-call | flops 800000000 | bytes 7274504 | tf_op jit(solution)/shard_map/first_update/pallas_call | solution.py:305
  131.3 2.7 %collective-permute-start.25 = (f32[128,256]{1,0:T(8,128)}, f32[128,256]{1,0:T(8,128)}, u32[]{:S(2)}, u32[]{:S(2)}) collective-permute-start(f32[128,256]{1,0:T(8,128)} %get-tuple-element.78), channel_id=1, source_target_pairs={{0,8},{8,0},{16,24},{24,16},{1,9},{9,1},{17,25},{25,17},{2,10},{10... | collective-permute-start | bytes 393224 | tf_op jit(solution)/shard_map/ppermute | solution.py:13
  134.0 5.0 %all-to-all-start.4 = ((f32[8,32,128]{2,1,0:T(8,128)}), f32[8,32,128]{2,1,0:T(8,128)}, u32[]{:S(2)}, u32[]{:S(2)}) async-start(f32[8,32,128]{2,1,0:T(8,128)} %copy-done.38), calls=%async_computation.4 | async-start | bytes 262144 | tf_op jit(solution)/shard_map/all_to_all | solution.py:366
  140.1 2.1 collective-permute-start.26
  142.1 4.5 %collective-permute-done.26 = f32[128,256]{1,0:T(8,128)S(1)} collective-permute-done((f32[128,256]{1,0:T(8,128)S(1)}, f32[128,256]{1,0:T(8,128)S(1)}, u32[]{:S(2)}, u32[]{:S(2)}) %collective-permute-start.26) | collective-permute-done | bytes 131104 | tf_op jit(solution)/shard_map/ppermute | solution.py:13
  148.1 1.0 copy-done.20
  150.7 1.0 copy-done.25
  151.8 1.4 coarse_part.5
  153.1 1.5 collective-permute-start.30
  156.1 1.0 add.86
  157.1 3.3 %collective-permute-start.28 = (f32[128,256]{1,0:T(8,128)S(1)}, f32[128,256]{1,0:T(8,128)S(1)}, u32[]{:S(2)}, u32[]{:S(2)}) collective-permute-start(f32[128,256]{1,0:T(8,128)S(1)} %add.86), channel_id=1, source_target_pairs={{0,2},{1,3},{2,0},{3,1},{4,6},{5,7},{6,4},{7,5},{8,10},{9,11},{10,... | collective-permute-start | bytes 393224 | tf_op jit(solution)/shard_map/ppermute | solution.py:13
  160.5 1.6 copy-done.4
  162.1 1.6 operator.5
  163.7 2.6 %collective-permute-start.34 = (f32[256,128]{1,0:T(8,128)S(1)}, f32[256,128]{1,0:T(8,128)S(1)}, u32[]{:S(2)}, u32[]{:S(2)}) collective-permute-start(f32[256,128]{1,0:T(8,128)S(1)} %get-tuple-element.90.refs_0_), channel_id=1, source_target_pairs={{0,1},{2,3},{4,5},{6,7},{1,0},{3,2},{5,4},{7,6},{8,9},{10,11},{12,... | collective-permute-start | bytes 393224 | tf_op jit(solution)/shard_map/ppermute | solution.py:324
  166.3 2.2 %collective-permute-start.29 = (f32[128,256]{1,0:T(8,128)S(1)}, f32[128,256]{1,0:T(8,128)S(1)}, u32[]{:S(2)}, u32[]{:S(2)}) collective-permute-start(f32[128,256]{1,0:T(8,128)S(1)} %add.87), channel_id=1, source_target_pairs={{0,4},{1,5},{2,6},{3,7},{4,0},{5,1},{6,2},{7,3},{8,12},{9,13},{10,... | collective-permute-start | bytes 393224 | tf_op jit(solution)/shard_map/ppermute | solution.py:13
  169.2 2.5 %collective-permute-start.36 = (f32[256,128]{1,0:T(8,128)S(1)}, f32[256,128]{1,0:T(8,128)S(1)}, u32[]{:S(2)}, u32[]{:S(2)}) collective-permute-start(f32[256,128]{1,0:T(8,128)S(1)} %get-tuple-element.92.refs_2_), channel_id=1, source_target_pairs={{0,8},{16,24},{8,0},{24,16},{1,9},{17,25},{9,1},{25,17},{2,10},{18... | collective-permute-start | bytes 393224 | tf_op jit(solution)/shard_map/ppermute | solution.py:324
  172.6 3.9 %inner_inverse.2 = f32[128,128]{1,0:T(8,128)S(1)} custom-call(f32[128,256]{1,0:T(8,128)S(1)} %copy-done.29), custom_call_target="tpu_custom_call" | custom-call | flops 400000000 | bytes 196608 | tf_op jit(solution)/shard_map/inner_inverse/pallas_call | solution.py:305
  176.7 6.9 %next_update.1 = (f32[1024,128]{1,0:T(8,128)S(1)}, f32[1024,128]{1,0:T(8,128)S(1)}, f32[1024,128]{1,0:T(8,128)S(1)}, f32[1024,128]{1,0:T(8,128)S(1)}, f32[1024,1...) custom-call(s32[2]{0:T(128)S(1)} %pad_add_fusion.parity, ...), custom_call_target="tpu_custom_call" | custom-call | flops 800000000 | bytes 11665416 | tf_op jit(solution)/shard_map/next_update/pallas_call | solution.py:305
  183.5 2.5 %collective-permute-start.38 = (f32[128,256]{1,0:T(8,128)S(1)}, f32[128,256]{1,0:T(8,128)S(1)}, u32[]{:S(2)}, u32[]{:S(2)}) collective-permute-start(f32[128,256]{1,0:T(8,128)S(1)} %get-tuple-element.94), channel_id=1, source_target_pairs={{0,8},{8,0},{16,24},{24,16},{1,9},{9,1},{17,25},{25,17},{2,10},{10... | collective-permute-start | bytes 393224 | tf_op jit(solution)/shard_map/ppermute | solution.py:13
  187.1 2.7 %collective-permute-start.39 = (f32[128,256]{1,0:T(8,128)S(1)}, f32[128,256]{1,0:T(8,128)S(1)}, u32[]{:S(2)}, u32[]{:S(2)}) collective-permute-start(f32[128,256]{1,0:T(8,128)S(1)} %add.89), channel_id=1, source_target_pairs={{0,1},{1,0},{2,3},{3,2},{4,5},{5,4},{6,7},{7,6},{8,9},{9,8},{10,11... | collective-permute-start | bytes 393224 | tf_op jit(solution)/shard_map/ppermute | solution.py:13
  189.8 4.0 %collective-permute-done.39 = f32[128,256]{1,0:T(8,128)S(1)} collective-permute-done((f32[128,256]{1,0:T(8,128)S(1)}, f32[128,256]{1,0:T(8,128)S(1)}, u32[]{:S(2)}, u32[]{:S(2)}) %collective-permute-start.39) | collective-permute-done | bytes 131104 | tf_op jit(solution)/shard_map/ppermute | solution.py:13
  194.1 5.0 %collective-permute-done.40 = f32[128,256]{1,0:T(8,128)S(1)} collective-permute-done((f32[128,256]{1,0:T(8,128)S(1)}, f32[128,256]{1,0:T(8,128)S(1)}, u32[]{:S(2)}, u32[]{:S(2)}) %collective-permute-start.40) | collective-permute-done | bytes 131104 | tf_op jit(solution)/shard_map/ppermute | solution.py:13
  199.1 2.1 collective-permute-start.41
  201.2 2.9 %collective-permute-done.41 = f32[128,256]{1,0:T(8,128)S(1)} collective-permute-done((f32[128,256]{1,0:T(8,128)S(1)}, f32[128,256]{1,0:T(8,128)S(1)}, u32[]{:S(2)}, u32[]{:S(2)}) %collective-permute-start.41) | collective-permute-done | bytes 131104 | tf_op jit(solution)/shard_map/ppermute | solution.py:13
  204.2 3.0 %collective-permute-start.42 = (f32[128,256]{1,0:T(8,128)S(1)}, f32[128,256]{1,0:T(8,128)S(1)}, u32[]{:S(2)}, u32[]{:S(2)}) collective-permute-start(f32[128,256]{1,0:T(8,128)S(1)} %add.92), channel_id=1, source_target_pairs={{0,4},{1,5},{2,6},{3,7},{4,0},{5,1},{6,2},{7,3},{8,12},{9,13},{10,... | collective-permute-start | bytes 393224 | tf_op jit(solution)/shard_map/ppermute | solution.py:13
  207.2 4.2 %inner_inverse.3 = f32[128,128]{1,0:T(8,128)S(1)} custom-call(f32[128,256]{1,0:T(8,128)S(1)} %add.88.grams), custom_call_target="tpu_custom_call" | custom-call | flops 400000000 | bytes 196608 | tf_op jit(solution)/shard_map/inner_inverse/pallas_call | solution.py:305
  211.4 5.8 %last_update.1 = (f32[1024,128]{1,0:T(8,128)}, f32[1024,128]{1,0:T(8,128)}) custom-call(f32[128,256]{1,0:T(8,128)S(1)} %add.93.grams, f32[128,128]{1,0:T(8,128)S(1)} %inner_inverse.3, f32[128,128]{1,0:T(8,128)S(1)} %get-tuple-element.95.curvature, f32[1024,128]{1,0:T(8,128)S(1)} %get-tuple-element.96.z, f32[1024,128]{1,0:T(8,128)S(1)} %get-tuple-element.97.w, ...), custom_call_target="tpu_custom_call" | custom-call | flops 800000000 | bytes 4456448 | tf_op jit(solution)/shard_map/last_update/pallas_call | solution.py:305
  (160 shorter events, 33.4 us)
Async XLA Ops:
  0.6 16.3 %copy-start = (bf16[1,128,1024]{2,1,0:T(8,128)(2,1)S(1)}, bf16[1,128,1024]{2,1,0:T(8,128)(2,1)}, u32[]{:S(2)}) copy-start(bf16[1,128,1024]{2,1,0:T(8,128)(2,1)} %param.13) | copy-start | bytes 786436
  0.6 28.5 %copy-start.16 = (bf16[1,1,32,1024]{3,2,1,0:T(8,128)(2,1)S(1)}, bf16[1,1,32,1024]{3,2,1,0:T(8,128)(2,1)}, u32[]{:S(2)}) copy-start(bf16[1,1,32,1024]{3,2,1,0:T(8,128)(2,1)} %param.11) | copy-start | bytes 196612
  1.9 13.7 %all-to-all-start = ((s32[8,1,32]{2,1,0:T(1,128)}), s32[8,1,32]{2,1,0:T(1,128)S(1)}, u32[]{:S(2)}, u32[]{:S(2)}) async-start(s32[8,1,32]{2,1,0:T(1,128)} %broadcast_in_dim.6), calls=%async_computation | async-start | bytes 8192 | tf_op jit(solution)/shard_map/all_to_all | solution.py:39
  16.9 22.4 %copy-start.1 = (bf16[1,1,1024,1024]{3,2,1,0:T(8,128)(2,1)S(1)}, bf16[1,1,1024,1024]{3,2,1,0:T(8,128)(2,1)}, u32[]{:S(2)}) copy-start(bf16[1,1,1024,1024]{3,2,1,0:T(8,128)(2,1)} %param.9) | copy-start | bytes 6291460
  18.1 13.7 %all-to-all-start.1 = ((bf16[8,32,256]{2,1,0:T(8,128)(2,1)}), bf16[8,32,256]{2,1,0:T(8,128)(2,1)}, u32[]{:S(2)}, u32[]{:S(2)}) async-start(bf16[8,32,256]{2,1,0:T(8,128)(2,1)} %bitcast.8), calls=%async_computation.1 | async-start | bytes 262144 | tf_op jit(solution)/shard_map/all_to_all | solution.py:60
  23.1 6.0 %collective-permute-start = (bf16[256,128]{1,0:T(8,128)(2,1)S(1)}, bf16[256,128]{1,0:T(8,128)(2,1)S(1)}, u32[]{:S(2)}, u32[]{:S(2)}) collective-permute-start(bf16[256,128]{1,0:T(8,128)(2,1)S(1)} %get-tuple-element.106.refs_0_), channel_id=1, source_target_pairs={{0,1},{2,3},{4,5},{6,7},{1,0},{3,2},{5,4},{7,6},{8,9},{10,11},{12,... | collective-permute-start | bytes 196616 | tf_op jit(solution)/shard_map/ppermute | solution.py:324
  25.0 4.1 %collective-permute-start.1 = (bf16[256,128]{1,0:T(8,128)(2,1)S(1)}, bf16[256,128]{1,0:T(8,128)(2,1)S(1)}, u32[]{:S(2)}, u32[]{:S(2)}) collective-permute-start(bf16[256,128]{1,0:T(8,128)(2,1)S(1)} %get-tuple-element.105.refs_1_), channel_id=1, source_target_pairs={{1,2},{3,4},{5,6},{2,1},{4,3},{6,5},{9,10},{11,12},{13,14},{10,9},... | collective-permute-start | bytes 196616 | tf_op jit(solution)/shard_map/ppermute | solution.py:324
  25.7 3.5 %collective-permute-start.2 = (bf16[256,128]{1,0:T(8,128)(2,1)S(1)}, bf16[256,128]{1,0:T(8,128)(2,1)S(1)}, u32[]{:S(2)}, u32[]{:S(2)}) collective-permute-start(bf16[256,128]{1,0:T(8,128)(2,1)S(1)} %get-tuple-element.107.refs_2_), channel_id=1, source_target_pairs={{0,8},{16,24},{8,0},{24,16},{1,9},{17,25},{9,1},{25,17},{2,10},{18... | collective-permute-start | bytes 196616 | tf_op jit(solution)/shard_map/ppermute | solution.py:324
  25.8 3.4 %collective-permute-start.3 = (bf16[256,128]{1,0:T(8,128)(2,1)S(1)}, bf16[256,128]{1,0:T(8,128)(2,1)S(1)}, u32[]{:S(2)}, u32[]{:S(2)}) collective-permute-start(bf16[256,128]{1,0:T(8,128)(2,1)S(1)} %get-tuple-element.104.refs_3_), channel_id=1, source_target_pairs={{8,16},{16,8},{9,17},{17,9},{10,18},{18,10},{11,19},{19,11},{12,20... | collective-permute-start | bytes 196616 | tf_op jit(solution)/shard_map/ppermute | solution.py:324
  31.8 15.0 %all-to-all-start.2 = ((f32[8,32,128]{2,1,0:T(8,128)}), f32[8,32,128]{2,1,0:T(8,128)}, u32[]{:S(2)}, u32[]{:S(2)}) async-start(f32[8,32,128]{2,1,0:T(8,128)} %copy-done.40), calls=%async_computation.2 | async-start | bytes 262144 | tf_op jit(solution)/shard_map/all_to_all | solution.py:366
  47.8 21.3 %copy-start.14 = (f32[1024,128]{1,0:T(8,128)S(1)}, f32[1024,128]{1,0:T(8,128)}, u32[]{:S(2)}) copy-start(f32[1024,128]{1,0:T(8,128)} %copy-done.12) | copy-start | bytes 1572868
  49.2 6.2 %collective-permute-start.4 = (f32[256,128]{1,0:T(8,128)S(1)}, f32[256,128]{1,0:T(8,128)S(1)}, u32[]{:S(2)}, u32[]{:S(2)}) collective-permute-start(f32[256,128]{1,0:T(8,128)S(1)} %get-tuple-element.57.refs_0_), channel_id=1, source_target_pairs={{0,1},{2,3},{4,5},{6,7},{1,0},{3,2},{5,4},{7,6},{8,9},{10,11},{12,... | collective-permute-start | bytes 393224 | tf_op jit(solution)/shard_map/ppermute | solution.py:324
  49.5 5.9 %collective-permute-start.5 = (f32[256,128]{1,0:T(8,128)S(1)}, f32[256,128]{1,0:T(8,128)S(1)}, u32[]{:S(2)}, u32[]{:S(2)}) collective-permute-start(f32[256,128]{1,0:T(8,128)S(1)} %get-tuple-element.58.refs_1_), channel_id=1, source_target_pairs={{1,2},{3,4},{5,6},{2,1},{4,3},{6,5},{9,10},{11,12},{13,14},{10,9},... | collective-permute-start | bytes 393224 | tf_op jit(solution)/shard_map/ppermute | solution.py:324
  50.1 5.3 %collective-permute-start.6 = (f32[256,128]{1,0:T(8,128)S(1)}, f32[256,128]{1,0:T(8,128)S(1)}, u32[]{:S(2)}, u32[]{:S(2)}) collective-permute-start(f32[256,128]{1,0:T(8,128)S(1)} %get-tuple-element.59.refs_2_), channel_id=1, source_target_pairs={{0,8},{16,24},{8,0},{24,16},{1,9},{17,25},{9,1},{25,17},{2,10},{18... | collective-permute-start | bytes 393224 | tf_op jit(solution)/shard_map/ppermute | solution.py:324
  51.2 4.2 %collective-permute-start.7 = (f32[256,128]{1,0:T(8,128)S(1)}, f32[256,128]{1,0:T(8,128)S(1)}, u32[]{:S(2)}, u32[]{:S(2)}) collective-permute-start(f32[256,128]{1,0:T(8,128)S(1)} %get-tuple-element.60.refs_3_), channel_id=1, source_target_pairs={{8,16},{16,8},{9,17},{17,9},{10,18},{18,10},{11,19},{19,11},{12,20... | collective-permute-start | bytes 393224 | tf_op jit(solution)/shard_map/ppermute | solution.py:324
  58.6 8.2 %collective-permute-start.10 = (f32[256,128]{1,0:T(8,128)S(1)}, f32[256,128]{1,0:T(8,128)S(1)}, u32[]{:S(2)}, u32[]{:S(2)}) collective-permute-start(f32[256,128]{1,0:T(8,128)S(1)} %get-tuple-element.64.refs_2_), channel_id=1, source_target_pairs={{0,8},{16,24},{8,0},{24,16},{1,9},{17,25},{9,1},{25,17},{2,10},{18... | collective-permute-start | bytes 393224 | tf_op jit(solution)/shard_map/ppermute | solution.py:324
  61.6 5.2 %collective-permute-start.11 = (f32[256,128]{1,0:T(8,128)S(1)}, f32[256,128]{1,0:T(8,128)S(1)}, u32[]{:S(2)}, u32[]{:S(2)}) collective-permute-start(f32[256,128]{1,0:T(8,128)S(1)} %get-tuple-element.65.refs_3_), channel_id=1, source_target_pairs={{8,16},{16,8},{9,17},{17,9},{10,18},{18,10},{11,19},{19,11},{12,20... | collective-permute-start | bytes 393224 | tf_op jit(solution)/shard_map/ppermute | solution.py:324
  62.3 6.8 %collective-permute-start.8 = (f32[256,128]{1,0:T(8,128)S(1)}, f32[256,128]{1,0:T(8,128)S(1)}, u32[]{:S(2)}, u32[]{:S(2)}) collective-permute-start(f32[256,128]{1,0:T(8,128)S(1)} %get-tuple-element.62.refs_0_), channel_id=1, source_target_pairs={{0,1},{2,3},{4,5},{6,7},{1,0},{3,2},{5,4},{7,6},{8,9},{10,11},{12,... | collective-permute-start | bytes 393224 | tf_op jit(solution)/shard_map/ppermute | solution.py:324
  66.1 3.0 %collective-permute-start.9 = (f32[256,128]{1,0:T(8,128)S(1)}, f32[256,128]{1,0:T(8,128)S(1)}, u32[]{:S(2)}, u32[]{:S(2)}) collective-permute-start(f32[256,128]{1,0:T(8,128)S(1)} %get-tuple-element.63.refs_1_), channel_id=1, source_target_pairs={{1,2},{3,4},{5,6},{2,1},{4,3},{6,5},{9,10},{11,12},{13,14},{10,9},... | collective-permute-start | bytes 393224 | tf_op jit(solution)/shard_map/ppermute | solution.py:324
  72.6 9.8 %collective-permute-start.12 = (f32[128,256]{1,0:T(8,128)}, f32[128,256]{1,0:T(8,128)}, u32[]{:S(2)}, u32[]{:S(2)}) collective-permute-start(f32[128,256]{1,0:T(8,128)} %get-tuple-element.66), channel_id=1, source_target_pairs={{0,8},{8,0},{16,24},{24,16},{1,9},{9,1},{17,25},{25,17},{2,10},{10... | collective-permute-start | bytes 393224 | tf_op jit(solution)/shard_map/ppermute | solution.py:13
  75.7 19.1 %all-to-all-start.3 = ((f32[8,32,128]{2,1,0:T(8,128)}), f32[8,32,128]{2,1,0:T(8,128)}, u32[]{:S(2)}, u32[]{:S(2)}) async-start(f32[8,32,128]{2,1,0:T(8,128)} %copy-done.39), calls=%async_computation.3 | async-start | bytes 262144 | tf_op jit(solution)/shard_map/all_to_all | solution.py:366
  83.5 6.3 %collective-permute-start.13 = (f32[128,256]{1,0:T(8,128)S(1)}, f32[128,256]{1,0:T(8,128)S(1)}, u32[]{:S(2)}, u32[]{:S(2)}) collective-permute-start(f32[128,256]{1,0:T(8,128)S(1)} %add.79), channel_id=1, source_target_pairs={{0,1},{1,0},{2,3},{3,2},{4,5},{5,4},{6,7},{7,6},{8,9},{9,8},{10,11... | collective-permute-start | bytes 393224 | tf_op jit(solution)/shard_map/ppermute | solution.py:13
  90.4 9.7 %collective-permute-start.14 = (f32[128,256]{1,0:T(8,128)}, f32[128,256]{1,0:T(8,128)}, u32[]{:S(2)}, u32[]{:S(2)}) collective-permute-start(f32[128,256]{1,0:T(8,128)} %add.80), channel_id=1, source_target_pairs={{0,16},{8,24},{16,0},{24,8},{1,17},{9,25},{17,1},{25,9},{2,18},{10... | collective-permute-start | bytes 393224 | tf_op jit(solution)/shard_map/ppermute | solution.py:13
  97.3 7.3 %collective-permute-start.17 = (f32[256,128]{1,0:T(8,128)S(1)}, f32[256,128]{1,0:T(8,128)S(1)}, u32[]{:S(2)}, u32[]{:S(2)}) collective-permute-start(f32[256,128]{1,0:T(8,128)S(1)} %get-tuple-element.69.refs_0_), channel_id=1, source_target_pairs={{0,1},{2,3},{4,5},{6,7},{1,0},{3,2},{5,4},{7,6},{8,9},{10,11},{12,... | collective-permute-start | bytes 393224 | tf_op jit(solution)/shard_map/ppermute | solution.py:324
  98.6 5.9 %collective-permute-start.18 = (f32[256,128]{1,0:T(8,128)S(1)}, f32[256,128]{1,0:T(8,128)S(1)}, u32[]{:S(2)}, u32[]{:S(2)}) collective-permute-start(f32[256,128]{1,0:T(8,128)S(1)} %get-tuple-element.70.refs_1_), channel_id=1, source_target_pairs={{1,2},{3,4},{5,6},{2,1},{4,3},{6,5},{9,10},{11,12},{13,14},{10,9},... | collective-permute-start | bytes 393224 | tf_op jit(solution)/shard_map/ppermute | solution.py:324
  99.3 5.2 %collective-permute-start.19 = (f32[256,128]{1,0:T(8,128)S(1)}, f32[256,128]{1,0:T(8,128)S(1)}, u32[]{:S(2)}, u32[]{:S(2)}) collective-permute-start(f32[256,128]{1,0:T(8,128)S(1)} %get-tuple-element.71.refs_2_), channel_id=1, source_target_pairs={{0,8},{16,24},{8,0},{24,16},{1,9},{17,25},{9,1},{25,17},{2,10},{18... | collective-permute-start | bytes 393224 | tf_op jit(solution)/shard_map/ppermute | solution.py:324
  99.4 5.2 %collective-permute-start.20 = (f32[256,128]{1,0:T(8,128)S(1)}, f32[256,128]{1,0:T(8,128)S(1)}, u32[]{:S(2)}, u32[]{:S(2)}) collective-permute-start(f32[256,128]{1,0:T(8,128)S(1)} %get-tuple-element.72.refs_3_), channel_id=1, source_target_pairs={{8,16},{16,8},{9,17},{17,9},{10,18},{18,10},{11,19},{19,11},{12,20... | collective-permute-start | bytes 393224 | tf_op jit(solution)/shard_map/ppermute | solution.py:324
  101.1 9.3 %collective-permute-start.15 = (f32[128,256]{1,0:T(8,128)S(1)}, f32[128,256]{1,0:T(8,128)S(1)}, u32[]{:S(2)}, u32[]{:S(2)}) collective-permute-start(f32[128,256]{1,0:T(8,128)S(1)} %add.81), channel_id=1, source_target_pairs={{0,2},{1,3},{2,0},{3,1},{4,6},{5,7},{6,4},{7,5},{8,10},{9,11},{10,... | collective-permute-start | bytes 393224 | tf_op jit(solution)/shard_map/ppermute | solution.py:13
  106.2 13.4 %copy-start.7 = (f32[1024,128]{1,0:T(8,128)S(1)}, f32[1024,128]{1,0:T(8,128)}, u32[]{:S(2)}) copy-start(f32[1024,128]{1,0:T(8,128)} %copy-done.5) | copy-start | bytes 1572868
  106.2 13.4 %copy-start.10 = (f32[1024,128]{1,0:T(8,128)S(1)}, f32[1024,128]{1,0:T(8,128)}, u32[]{:S(2)}) copy-start(f32[1024,128]{1,0:T(8,128)} %copy-done.9) | copy-start | bytes 1572868
  106.2 13.4 %copy-start.15 = (f32[1024,128]{1,0:T(8,128)S(1)}, f32[1024,128]{1,0:T(8,128)}, u32[]{:S(2)}) copy-start(f32[1024,128]{1,0:T(8,128)} %copy-done.12) | copy-start | bytes 1572868
  107.7 19.0 %copy-start.17 = (f32[1024,128]{1,0:T(8,128)}, f32[1024,128]{1,0:T(8,128)S(1)}, u32[]{:S(2)}) copy-start(f32[1024,128]{1,0:T(8,128)S(1)} %get-tuple-element.73.m.q) | copy-start | bytes 1572868
  107.7 11.8 %collective-permute-start.21 = (f32[256,128]{1,0:T(8,128)S(1)}, f32[256,128]{1,0:T(8,128)S(1)}, u32[]{:S(2)}, u32[]{:S(2)}) collective-permute-start(f32[256,128]{1,0:T(8,128)S(1)} %get-tuple-element.74.refs_0_), channel_id=1, source_target_pairs={{0,1},{2,3},{4,5},{6,7},{1,0},{3,2},{5,4},{7,6},{8,9},{10,11},{12,... | collective-permute-start | bytes 393224 | tf_op jit(solution)/shard_map/ppermute | solution.py:324
  110.4 9.1 %collective-permute-start.16 = (f32[128,256]{1,0:T(8,128)S(1)}, f32[128,256]{1,0:T(8,128)S(1)}, u32[]{:S(2)}, u32[]{:S(2)}) collective-permute-start(f32[128,256]{1,0:T(8,128)S(1)} %add.82), channel_id=1, source_target_pairs={{0,4},{1,5},{2,6},{3,7},{4,0},{5,1},{6,2},{7,3},{8,12},{9,13},{10,... | collective-permute-start | bytes 393224 | tf_op jit(solution)/shard_map/ppermute | solution.py:13
  112.7 6.8 %collective-permute-start.22 = (f32[256,128]{1,0:T(8,128)S(1)}, f32[256,128]{1,0:T(8,128)S(1)}, u32[]{:S(2)}, u32[]{:S(2)}) collective-permute-start(f32[256,128]{1,0:T(8,128)S(1)} %get-tuple-element.75.refs_1_), channel_id=1, source_target_pairs={{1,2},{3,4},{5,6},{2,1},{4,3},{6,5},{9,10},{11,12},{13,14},{10,9},... | collective-permute-start | bytes 393224 | tf_op jit(solution)/shard_map/ppermute | solution.py:324
  113.3 6.2 %collective-permute-start.23 = (f32[256,128]{1,0:T(8,128)S(1)}, f32[256,128]{1,0:T(8,128)S(1)}, u32[]{:S(2)}, u32[]{:S(2)}) collective-permute-start(f32[256,128]{1,0:T(8,128)S(1)} %get-tuple-element.76.refs_2_), channel_id=1, source_target_pairs={{0,8},{16,24},{8,0},{24,16},{1,9},{17,25},{9,1},{25,17},{2,10},{18... | collective-permute-start | bytes 393224 | tf_op jit(solution)/shard_map/ppermute | solution.py:324
  116.0 3.6 %collective-permute-start.24 = (f32[256,128]{1,0:T(8,128)S(1)}, f32[256,128]{1,0:T(8,128)S(1)}, u32[]{:S(2)}, u32[]{:S(2)}) collective-permute-start(f32[256,128]{1,0:T(8,128)S(1)} %get-tuple-element.77.refs_3_), channel_id=1, source_target_pairs={{8,16},{16,8},{9,17},{17,9},{10,18},{18,10},{11,19},{19,11},{12,20... | collective-permute-start | bytes 393224 | tf_op jit(solution)/shard_map/ppermute | solution.py:324
  131.3 7.8 %collective-permute-start.25 = (f32[128,256]{1,0:T(8,128)}, f32[128,256]{1,0:T(8,128)}, u32[]{:S(2)}, u32[]{:S(2)}) collective-permute-start(f32[128,256]{1,0:T(8,128)} %get-tuple-element.78), channel_id=1, source_target_pairs={{0,8},{8,0},{16,24},{24,16},{1,9},{9,1},{17,25},{25,17},{2,10},{10... | collective-permute-start | bytes 393224 | tf_op jit(solution)/shard_map/ppermute | solution.py:13
  134.0 16.7 %all-to-all-start.4 = ((f32[8,32,128]{2,1,0:T(8,128)}), f32[8,32,128]{2,1,0:T(8,128)}, u32[]{:S(2)}, u32[]{:S(2)}) async-start(f32[8,32,128]{2,1,0:T(8,128)} %copy-done.38), calls=%async_computation.4 | async-start | bytes 262144 | tf_op jit(solution)/shard_map/all_to_all | solution.py:366
  140.1 6.6 %collective-permute-start.26 = (f32[128,256]{1,0:T(8,128)S(1)}, f32[128,256]{1,0:T(8,128)S(1)}, u32[]{:S(2)}, u32[]{:S(2)}) collective-permute-start(f32[128,256]{1,0:T(8,128)S(1)} %add.84), channel_id=1, source_target_pairs={{0,1},{1,0},{2,3},{3,2},{4,5},{5,4},{6,7},{7,6},{8,9},{9,8},{10,11... | collective-permute-start | bytes 393224 | tf_op jit(solution)/shard_map/ppermute | solution.py:13
  147.4 8.7 %collective-permute-start.27 = (f32[128,256]{1,0:T(8,128)}, f32[128,256]{1,0:T(8,128)}, u32[]{:S(2)}, u32[]{:S(2)}) collective-permute-start(f32[128,256]{1,0:T(8,128)} %add.85), channel_id=1, source_target_pairs={{0,16},{8,24},{16,0},{24,8},{1,17},{9,25},{17,1},{25,9},{2,18},{10... | collective-permute-start | bytes 393224 | tf_op jit(solution)/shard_map/ppermute | solution.py:13
  153.1 7.3 %collective-permute-start.30 = (f32[256,128]{1,0:T(8,128)S(1)}, f32[256,128]{1,0:T(8,128)S(1)}, u32[]{:S(2)}, u32[]{:S(2)}) collective-permute-start(f32[256,128]{1,0:T(8,128)S(1)} %get-tuple-element.83.refs_0_), channel_id=1, source_target_pairs={{0,1},{2,3},{4,5},{6,7},{1,0},{3,2},{5,4},{7,6},{8,9},{10,11},{12,... | collective-permute-start | bytes 393224 | tf_op jit(solution)/shard_map/ppermute | solution.py:324
  154.6 5.8 %collective-permute-start.31 = (f32[256,128]{1,0:T(8,128)S(1)}, f32[256,128]{1,0:T(8,128)S(1)}, u32[]{:S(2)}, u32[]{:S(2)}) collective-permute-start(f32[256,128]{1,0:T(8,128)S(1)} %get-tuple-element.84.refs_1_), channel_id=1, source_target_pairs={{1,2},{3,4},{5,6},{2,1},{4,3},{6,5},{9,10},{11,12},{13,14},{10,9},... | collective-permute-start | bytes 393224 | tf_op jit(solution)/shard_map/ppermute | solution.py:324
  155.3 5.1 %collective-permute-start.32 = (f32[256,128]{1,0:T(8,128)S(1)}, f32[256,128]{1,0:T(8,128)S(1)}, u32[]{:S(2)}, u32[]{:S(2)}) collective-permute-start(f32[256,128]{1,0:T(8,128)S(1)} %get-tuple-element.85.refs_2_), channel_id=1, source_target_pairs={{0,8},{16,24},{8,0},{24,16},{1,9},{17,25},{9,1},{25,17},{2,10},{18... | collective-permute-start | bytes 393224 | tf_op jit(solution)/shard_map/ppermute | solution.py:324
  155.4 5.1 %collective-permute-start.33 = (f32[256,128]{1,0:T(8,128)S(1)}, f32[256,128]{1,0:T(8,128)S(1)}, u32[]{:S(2)}, u32[]{:S(2)}) collective-permute-start(f32[256,128]{1,0:T(8,128)S(1)} %get-tuple-element.86.refs_3_), channel_id=1, source_target_pairs={{8,16},{16,8},{9,17},{17,9},{10,18},{18,10},{11,19},{19,11},{12,20... | collective-permute-start | bytes 393224 | tf_op jit(solution)/shard_map/ppermute | solution.py:324
  156.1 16.5 %copy-start.29 = (f32[128,256]{1,0:T(8,128)S(1)}, f32[128,256]{1,0:T(8,128)}, u32[]{:S(2)}) copy-start(f32[128,256]{1,0:T(8,128)} %copy-done.28) | copy-start | bytes 393220
  157.1 9.2 %collective-permute-start.28 = (f32[128,256]{1,0:T(8,128)S(1)}, f32[128,256]{1,0:T(8,128)S(1)}, u32[]{:S(2)}, u32[]{:S(2)}) collective-permute-start(f32[128,256]{1,0:T(8,128)S(1)} %add.86), channel_id=1, source_target_pairs={{0,2},{1,3},{2,0},{3,1},{4,6},{5,7},{6,4},{7,5},{8,10},{9,11},{10,... | collective-permute-start | bytes 393224 | tf_op jit(solution)/shard_map/ppermute | solution.py:13
  162.1 14.5 %copy-start.31 = (f32[1024,128]{1,0:T(8,128)S(1)}, f32[1024,128]{1,0:T(8,128)}, u32[]{:S(2)}) copy-start(f32[1024,128]{1,0:T(8,128)} %copy-done.30) | copy-start | bytes 1572868
  162.1 14.5 %copy-start.33 = (f32[1024,128]{1,0:T(8,128)S(1)}, f32[1024,128]{1,0:T(8,128)}, u32[]{:S(2)}) copy-start(f32[1024,128]{1,0:T(8,128)} %copy-done.32) | copy-start | bytes 1572868
  162.1 14.5 %copy-start.35 = (f32[1024,128]{1,0:T(8,128)S(1)}, f32[1024,128]{1,0:T(8,128)}, u32[]{:S(2)}) copy-start(f32[1024,128]{1,0:T(8,128)} %copy-done.34) | copy-start | bytes 1572868
  162.1 14.5 %copy-start.37 = (f32[1024,128]{1,0:T(8,128)S(1)}, f32[1024,128]{1,0:T(8,128)}, u32[]{:S(2)}) copy-start(f32[1024,128]{1,0:T(8,128)} %copy-done.36) | copy-start | bytes 1572868
  163.7 13.0 %copy-start.8 = (f32[1024,128]{1,0:T(8,128)S(1)}, f32[1024,128]{1,0:T(8,128)}, u32[]{:S(2)}) copy-start(f32[1024,128]{1,0:T(8,128)} %copy-done.5) | copy-start | bytes 1572868
  163.7 13.0 %copy-start.11 = (f32[1024,128]{1,0:T(8,128)S(1)}, f32[1024,128]{1,0:T(8,128)}, u32[]{:S(2)}) copy-start(f32[1024,128]{1,0:T(8,128)} %copy-done.9) | copy-start | bytes 1572868
  163.7 13.0 %copy-start.18 = (f32[1024,128]{1,0:T(8,128)S(1)}, f32[1024,128]{1,0:T(8,128)}, u32[]{:S(2)}) copy-start(f32[1024,128]{1,0:T(8,128)} %copy-done.17) | copy-start | bytes 1572868
  163.7 12.8 %collective-permute-start.34 = (f32[256,128]{1,0:T(8,128)S(1)}, f32[256,128]{1,0:T(8,128)S(1)}, u32[]{:S(2)}, u32[]{:S(2)}) collective-permute-start(f32[256,128]{1,0:T(8,128)S(1)} %get-tuple-element.90.refs_0_), channel_id=1, source_target_pairs={{0,1},{2,3},{4,5},{6,7},{1,0},{3,2},{5,4},{7,6},{8,9},{10,11},{12,... | collective-permute-start | bytes 393224 | tf_op jit(solution)/shard_map/ppermute | solution.py:324
  166.3 10.2 %collective-permute-start.29 = (f32[128,256]{1,0:T(8,128)S(1)}, f32[128,256]{1,0:T(8,128)S(1)}, u32[]{:S(2)}, u32[]{:S(2)}) collective-permute-start(f32[128,256]{1,0:T(8,128)S(1)} %add.87), channel_id=1, source_target_pairs={{0,4},{1,5},{2,6},{3,7},{4,0},{5,1},{6,2},{7,3},{8,12},{9,13},{10,... | collective-permute-start | bytes 393224 | tf_op jit(solution)/shard_map/ppermute | solution.py:13
  168.5 8.0 %collective-permute-start.35 = (f32[256,128]{1,0:T(8,128)S(1)}, f32[256,128]{1,0:T(8,128)S(1)}, u32[]{:S(2)}, u32[]{:S(2)}) collective-permute-start(f32[256,128]{1,0:T(8,128)S(1)} %get-tuple-element.91.refs_1_), channel_id=1, source_target_pairs={{1,2},{3,4},{5,6},{2,1},{4,3},{6,5},{9,10},{11,12},{13,14},{10,9},... | collective-permute-start | bytes 393224 | tf_op jit(solution)/shard_map/ppermute | solution.py:324
  169.2 7.4 %collective-permute-start.36 = (f32[256,128]{1,0:T(8,128)S(1)}, f32[256,128]{1,0:T(8,128)S(1)}, u32[]{:S(2)}, u32[]{:S(2)}) collective-permute-start(f32[256,128]{1,0:T(8,128)S(1)} %get-tuple-element.92.refs_2_), channel_id=1, source_target_pairs={{0,8},{16,24},{8,0},{24,16},{1,9},{17,25},{9,1},{25,17},{2,10},{18... | collective-permute-start | bytes 393224 | tf_op jit(solution)/shard_map/ppermute | solution.py:324
  171.6 4.9 %collective-permute-start.37 = (f32[256,128]{1,0:T(8,128)S(1)}, f32[256,128]{1,0:T(8,128)S(1)}, u32[]{:S(2)}, u32[]{:S(2)}) collective-permute-start(f32[256,128]{1,0:T(8,128)S(1)} %get-tuple-element.93.refs_3_), channel_id=1, source_target_pairs={{8,16},{16,8},{9,17},{17,9},{10,18},{18,10},{11,19},{19,11},{12,20... | collective-permute-start | bytes 393224 | tf_op jit(solution)/shard_map/ppermute | solution.py:324
  183.5 3.5 %collective-permute-start.38 = (f32[128,256]{1,0:T(8,128)S(1)}, f32[128,256]{1,0:T(8,128)S(1)}, u32[]{:S(2)}, u32[]{:S(2)}) collective-permute-start(f32[128,256]{1,0:T(8,128)S(1)} %get-tuple-element.94), channel_id=1, source_target_pairs={{0,8},{8,0},{16,24},{24,16},{1,9},{9,1},{17,25},{25,17},{2,10},{10... | collective-permute-start | bytes 393224 | tf_op jit(solution)/shard_map/ppermute | solution.py:13
  187.1 6.7 %collective-permute-start.39 = (f32[128,256]{1,0:T(8,128)S(1)}, f32[128,256]{1,0:T(8,128)S(1)}, u32[]{:S(2)}, u32[]{:S(2)}) collective-permute-start(f32[128,256]{1,0:T(8,128)S(1)} %add.89), channel_id=1, source_target_pairs={{0,1},{1,0},{2,3},{3,2},{4,5},{5,4},{6,7},{7,6},{8,9},{9,8},{10,11... | collective-permute-start | bytes 393224 | tf_op jit(solution)/shard_map/ppermute | solution.py:13
  193.8 5.3 %collective-permute-start.40 = (f32[128,256]{1,0:T(8,128)S(1)}, f32[128,256]{1,0:T(8,128)S(1)}, u32[]{:S(2)}, u32[]{:S(2)}) collective-permute-start(f32[128,256]{1,0:T(8,128)S(1)} %add.90), channel_id=1, source_target_pairs={{0,16},{8,24},{16,0},{24,8},{1,17},{9,25},{17,1},{25,9},{2,18},{10... | collective-permute-start | bytes 393224 | tf_op jit(solution)/shard_map/ppermute | solution.py:13
  199.1 5.1 %collective-permute-start.41 = (f32[128,256]{1,0:T(8,128)S(1)}, f32[128,256]{1,0:T(8,128)S(1)}, u32[]{:S(2)}, u32[]{:S(2)}) collective-permute-start(f32[128,256]{1,0:T(8,128)S(1)} %add.91), channel_id=1, source_target_pairs={{0,2},{1,3},{2,0},{3,1},{4,6},{5,7},{6,4},{7,5},{8,10},{9,11},{10,... | collective-permute-start | bytes 393224 | tf_op jit(solution)/shard_map/ppermute | solution.py:13
  204.2 7.2 %collective-permute-start.42 = (f32[128,256]{1,0:T(8,128)S(1)}, f32[128,256]{1,0:T(8,128)S(1)}, u32[]{:S(2)}, u32[]{:S(2)}) collective-permute-start(f32[128,256]{1,0:T(8,128)S(1)} %add.92), channel_id=1, source_target_pairs={{0,4},{1,5},{2,6},{3,7},{4,0},{5,1},{6,2},{7,3},{8,12},{9,13},{10,... | collective-permute-start | bytes 393224 | tf_op jit(solution)/shard_map/ppermute | solution.py:13
  (27 other events, 55.1 us)
